TPU v7x, 32 devices: a whole 2x2x4 slice. The times are simulated.
32 devices in a mesh: group: 2 (over y), space: 8 (over z, core), member: 2 (over x), level: 1.
Axes of the slice: x: 2, y: 2, z: 4, core: 2. Of those that a mesh axis runs over, the one named last changes fastest.
Arguments:
- atm_state: bfloat16 [2, 256, 128, 128], P('member', ('group', 'space')), parts along dimension 1, may hold values from -6 to 6
- remap_tiles: bfloat16 [128, 4, 128, 128], P('space'), may hold values from -0.375 to 0.375
- dest_device: int32 [128, 4], P('space'), may hold values from 0 to 7, all different within a row; in each aligned block of 16 rows (0 to 15, 16 to 31, ...) at most 16 rows name the same one
- dest_block: int32 [128, 4], P('space'), may hold values from 0 to 31
- wet_mask: int32 [256, 128], P('space'), may hold values 0 or 1
- target: float32 [2, 512, 4, 128], P('member', ('group', 'space')), parts along dimension 1, may hold values from -6 to 6
- w_in: bfloat16 [128, 1024], P(None, 'level'), may hold values from -0.5 to 0.5
- w_out: bfloat16 [1024, 4], P('level'), may hold values from -0.375 to 0.375
Outputs:
- atm_adjoint: float32 [2, 256, 128, 128], P('member', ('group', 'space'), 'level'), parts along dimension 1
- grad_w_in: float32 [256, 1024], P('group', 'level'), parts along dimension 0
- grad_w_out: float32 [1024, 8], P('level', 'group'), parts along dimension 1
There are 2 independent parts, one for each index of `group`. A program takes and returns all parts, laid end to end along the dimension named above; an argument that names none is the same for every part. Nothing has to cross between parts.
Inputs may be any that keep to these rules, and one draw needn't show every extreme that they name: `dest_device`: among the 16 atmosphere blocks of one device, no owner is named more than 16 times, a bound that some block reaches; the 4 owners of one block are distinct.
All inputs are finite; a program needn't handle non-finite values. No bound on the sum of `wet_mask` on one device may be relied on, other than what follows from the above.
Results may differ from a plain program's by a relative error of at most 0.002.
The roundings to bfloat16 on the way count: a program that leaves them out, or rounds other values in their place, can miss the bound.
Values may be sent and summed in bfloat16 or wider, within the bound.
A program may use at most 64 MiB of HBM per device.

v0:
```python
import math

import jax
import jax.numpy as jnp
from jax import lax
from jax.sharding import PartitionSpec as P


def remap_pieces(source, remap_tiles, slot_index, slot_total):
    pieces = jnp.einsum(
        "aci,akij->akcj", source, remap_tiles, preferred_element_type=jnp.float32
    ).astype(jnp.bfloat16)
    pair_count = pieces.shape[0] * pieces.shape[1]
    pieces = pieces.reshape(pair_count, source.shape[1], source.shape[2])
    return (
        jnp.zeros((slot_total, source.shape[1], source.shape[2]), jnp.bfloat16)
        .at[slot_index]
        .set(pieces)
    )


def add_pieces(received, received_ids, ocean_blocks):
    flat_data = received.reshape(-1, received.shape[2], received.shape[3]).astype(jnp.float32)
    summed = jnp.zeros((ocean_blocks + 1, received.shape[2], received.shape[3]), jnp.float32)
    summed = summed.at[received_ids.reshape(-1)].add(flat_data)
    return summed[:ocean_blocks].astype(jnp.bfloat16)


def body(atm_state, remap_tiles, dest_device, dest_block, wet_mask, target, w_in, w_out):
    space_size = lax.axis_size("space")
    member_size = lax.axis_size("member")
    level_size = lax.axis_size("level")
    atm_blocks, top_count, cells, _ = remap_tiles.shape
    ocean_blocks = wet_mask.shape[0]
    channels = atm_state.shape[2]
    half_chan = channels // level_size
    capacity = min(atm_blocks, max(2, 2 * atm_blocks * top_count // space_size))
    pair_count = atm_blocks * top_count
    slot_total = space_size * capacity
    dest_flat = dest_device.reshape(pair_count)
    onehot = (dest_flat[:, None] == jnp.arange(space_size, dtype=jnp.int32)[None, :]).astype(
        jnp.int32
    )
    slot_rank = jnp.sum((jnp.cumsum(onehot, axis=0) - onehot) * onehot, axis=1)
    slot_index = dest_flat * capacity + slot_rank
    send_ids = (
        jnp.full((slot_total,), ocean_blocks, jnp.int32)
        .at[slot_index]
        .set(dest_block.reshape(pair_count))
    )
    send_ids = send_ids.reshape(space_size, capacity)
    local_state = atm_state[0]
    outgoing = remap_pieces(local_state, remap_tiles, slot_index, slot_total).reshape(
        space_size, capacity, channels, cells
    )
    received, received_ids = (
        lax.all_to_all(outgoing, "space", split_axis=0, concat_axis=0, tiled=True),
        lax.all_to_all(send_ids, "space", split_axis=0, concat_axis=0, tiled=True),
    )
    features = add_pieces(received, received_ids, ocean_blocks)
    pre_act = jnp.einsum("ch,ocj->ohj", w_in, features, preferred_element_type=jnp.float32)
    activated = jax.nn.silu(pre_act).astype(jnp.bfloat16)
    partial_flux = jnp.einsum("hq,ohj->oqj", w_out, activated, preferred_element_type=jnp.float32)
    predicted = lax.psum(partial_flux, "level")
    misfit = wet_mask.astype(jnp.float32)[:, None, :] * (predicted - target[0])
    act_grad = jnp.einsum(
        "hq,oqj->ohj", w_out.astype(jnp.float32), misfit, precision=lax.Precision.HIGHEST
    )
    gate_value = jax.nn.sigmoid(pre_act)
    pre_grad = (act_grad * gate_value * (1.0 + pre_act * (1.0 - gate_value))).astype(jnp.bfloat16)
    feat_grad = lax.psum_scatter(
        jnp.einsum("ch,ohj->coj", w_in, pre_grad, preferred_element_type=jnp.float32),
        "level",
        scatter_dimension=0,
        tiled=True,
    ).astype(jnp.bfloat16)
    reply = jnp.take(feat_grad, received_ids.reshape(-1), axis=1, mode="clip")
    reply = reply.reshape(half_chan, space_size, capacity, cells)
    returned = lax.all_to_all(reply, "space", split_axis=1, concat_axis=1, tiled=True)
    pair_grad = jnp.take(returned.reshape(half_chan, slot_total, cells), slot_index, axis=1)
    pair_grad = pair_grad.reshape(half_chan, atm_blocks, top_count, cells)
    adjoint = jnp.einsum(
        "cakj,akij->aci", pair_grad, remap_tiles, preferred_element_type=jnp.float32
    )
    cell_total = member_size * space_size * ocean_blocks * cells
    scale_in = math.sqrt(w_in.shape[1] * level_size / cell_total)
    scale_out = 1.0 / math.sqrt(cell_total)
    grad_in = scale_in * jnp.einsum(
        "ocj,ohj->ch", features, pre_grad, preferred_element_type=jnp.float32
    )
    grad_out = scale_out * jnp.einsum(
        "ohj,oqj->hq",
        activated,
        misfit,
        preferred_element_type=jnp.float32,
        precision=lax.Precision.HIGHEST,
    )
    grad_in, grad_out = lax.psum((grad_in, grad_out), ("space", "member"))
    return (adjoint[None], grad_in, grad_out)


def solution(mesh):
    return jax.shard_map(
        body,
        mesh=mesh,
        in_specs=(
            P("member", ("group", "space"), None, None),
            P("space", None, None, None),
            P("space", None),
            P("space", None),
            P("space", None),
            P("member", ("group", "space"), None, None),
            P(None, "level"),
            P("level", None),
        ),
        out_specs=(
            P("member", ("group", "space"), "level", None),
            P("group", "level"),
            P("level", "group"),
        ),
        check_vma=False,
    )
```

profile of v0, /device:TPU:0, one launch (start us, length us, event | category | flops | bytes accessed | tf_op | source)
XLA Modules:
  0.0 379.9 jit_solution(5706364221076013006)
XLA Ops:
  7.2 0.0 copy-start
  7.2 0.9 copy.30
  8.1 0.1 reshape.107
  8.2 0.1 mul.59
  8.3 0.8 copy.32
  9.0 0.1 reshape.135
  9.1 0.1 fusion.25
  9.2 0.1 reduce_window_sum.11
  9.3 0.2 select_reduce_fusion
  9.5 0.8 scatter_custom_fusion
  10.3 0.7 all_to_all.12
  11.0 6.3 %all-to-all-start = ((s32[8,1,16]{2,1,0:T(1,128)}), s32[8,1,16]{2,1,0:T(1,128)S(1)}, u32[]{:S(2)}, u32[]{:S(2)}) async-start(s32[8,1,16]{2,1,0:T(1,128)} %bitcast.2), calls=%async_computation | async-start | bytes 8192 | tf_op jit(solution)/shard_map/all_to_all | solution.py:58
  17.3 0.0 copy-done
  17.3 3.2 convolution_convert_fusion
  20.5 4.1 %copy.35 = bf16[64,128,128]{2,1,0:T(8,128)(2,1)} copy(bf16[64,128,128]{1,2,0:T(8,128)(2,1)} %bitcast.105) | data formatting | bytes 4194304 | tf_op jit(solution)/shard_map/reshape | solution.py:14
  24.5 3.0 broadcast_in_dim.32
  27.5 10.0 %scatter_fusion = bf16[128,128,128]{2,1,0:T(8,128)(2,1)} fusion(bf16[128,128,128]{2,1,0:T(8,128)(2,1)} %broadcast_in_dim.32, s32[64]{0:T(128)S(1)} %fusion.28, bf16[64,128,128]{2,1,0:T(8,128)(2,1)} %copy.35), kind=kCustom, calls=%fused_computation.3 | custom fusion | bytes 6291712 | tf_op jit(solution)/shard_map/scatter | solution.py:18
  37.5 0.0 all-to-all-done
  37.5 0.0 copy-start.6
  37.5 5.2 %all-to-all-start.1 = ((bf16[8,16,128,128]{3,2,1,0:T(8,128)(2,1)}), bf16[8,16,128,128]{3,2,1,0:T(8,128)(2,1)}, u32[]{:S(2)}, u32[]{:S(2)}) async-start(bf16[8,16,128,128]{3,2,1,0:T(8,128)(2,1)} %bitcast.102), calls=%async_computation.1 | async-start | bytes 8388608 | tf_op jit(solution)/shard_map/all_to_all | solution.py:57
  42.7 0.0 copy-done.6
  42.7 0.1 reshape.117
  42.8 0.5 broadcast.80
  43.3 0.7 reduce.5
  44.0 0.1 reshape.109
  44.1 92.7 %all-to-all-done.1 = bf16[8,16,128,128]{3,2,1,0:T(8,128)(2,1)} async-done(((bf16[8,16,128,128]{3,2,1,0:T(8,128)(2,1)}), bf16[8,16,128,128]{3,2,1,0:T(8,128)(2,1)}, u32[]{:S(2)}, u32[]{:S(2)}) %all-to-all-start.1) | async-done | bytes 4194336 | tf_op jit(solution)/shard_map/all_to_all | solution.py:57
  136.8 6.5 %bitcast_convert_fusion = f32[128,128,128]{2,1,0:T(8,128)} fusion(bf16[8,16,128,128]{3,2,1,0:T(8,128)(2,1)} %all-to-all-done.1), kind=kLoop, calls=%fused_computation.16 | loop fusion | flops 2097152 | bytes 12582912 | tf_op jit(solution)/shard_map/convert_element_type | solution.py:23
  143.3 1.6 broadcast_in_dim.30
  145.0 0.0 copy-start.8
  145.0 26.3 %scatter_fusion.1 = f32[33,128,128]{2,1,0:T(8,128)} fusion(f32[33,128,128]{2,1,0:T(8,128)} %broadcast_in_dim.30, s32[128]{0:T(128)S(1)} %fusion.29, f32[128,128,128]{2,1,0:T(8,128)} %bitcast_convert_fusion), kind=kCustom, calls=%fused_computation.4 | custom fusion | flops 2097152 | bytes 25166336 | tf_op jit(solution)/shard_map/scatter-add | solution.py:25
  171.3 2.1 copy.36
  173.4 0.0 copy-done.8
  173.4 0.0 copy-start.3
  173.4 0.0 copy-start.5
  173.4 0.0 copy-start.7
  173.4 8.4 %fusion.5 = (bf16[32,1024,128]{1,2,0:T(8,128)(2,1)S(1)}, f32[32,128,1024]{2,1,0:T(8,128)}) fusion(bf16[33,128,128]{1,2,0:T(8,128)(2,1)S(1)} %copy.36, bf16[128,1024]{1,0:T(8,128)(2,1)S(1)} %copy-done.8), kind=kOutput, calls=%fused_computation.14 | convolution fusion | flops 1094713344 | bytes 26509312 | tf_op jit(solution)/shard_map/ch,ocj->ohj/dot_general | solution.py:61
  181.8 0.0 copy-done.3
  181.8 0.0 copy-start.1
  181.8 0.0 copy-done.5
  181.8 0.0 copy-done.7
  181.8 2.3 fusion.16
  184.1 0.9 copy-done.1
  185.1 15.1 %fusion.1 = bf16[32,1024,128]{1,2,0:T(8,128)(2,1)S(1)} fusion(f32[32,128,1024]{2,1,0:T(8,128)} %get-tuple-element.4, f32[32,4,128]{2,1,0:T(4,128)S(1)} %fusion.16, bf16[1024,4]{0,1:T(4,128)(2,1)S(1)} %copy-done.7), kind=kOutput, calls=%fused_computation.7 | convolution fusion | flops 239075328 | bytes 25239552 | tf_op jit(solution)/shard_map/hq,oqj->ohj/dot_general | solution.py:66
  200.2 0.0 copy-start.2
  200.2 3.2 copy-done.2
  203.4 2.3 fusion.10
  205.8 3.0 gather_fusion
  208.8 0.0 copy-start.4
  208.8 4.7 %all-to-all-start.2 = ((bf16[128,8,16,128]{0,3,2,1:T(8,128)(2,1)}), bf16[128,8,16,128]{0,3,2,1:T(8,128)(2,1)}, u32[]{:S(2)}, u32[]{:S(2)}) async-start(bf16[128,8,16,128]{0,3,2,1:T(8,128)(2,1)} %bitcast.103), calls=%async_computation.2 | async-start | bytes 8388608 | tf_op jit(solution)/shard_map/all_to_all | solution.py:79
  213.6 0.0 all-reduce.2.cloned.1.call-start
  213.6 0.1 reduce_sum.14
  213.7 0.0 copy-done.4
  213.7 5.5 %fusion.14 = f32[128,1024]{1,0:T(8,128)} fusion(bf16[32,1024,128]{1,2,0:T(8,128)(2,1)} %copy-done.2, bf16[33,128,128]{1,2,0:T(8,128)(2,1)S(1)} %copy-done.4), kind=kOutput, calls=%fused_computation.25 | convolution fusion | flops 1073872896 | bytes 9994240 | tf_op jit(solution)/shard_map/ocj,ohj->ch/dot_general | solution.py:88
  219.2 0.0 all-reduce.2.cloned.1.call-update
  219.2 5.6 %fusion.17 = f32[1024,4]{0,1:T(4,128)S(1)} fusion(bf16[32,1024,128]{1,2,0:T(8,128)(2,1)} %copy-done.1, f32[32,4,128]{2,1,0:T(4,128)S(1)} %fusion.16), kind=kOutput, calls=%fused_computation.30 | convolution fusion | flops 201330688 | bytes 8470528 | tf_op jit(solution)/shard_map/ohj,oqj->hq/dot_general | solution.py:91
  224.9 132.2 %psum.18 = f32[1024,4]{0,1:T(4,128)} all-reduce(f32[1024,4]{0,1:T(4,128)S(1)} %fusion.17), channel_id=1, replica_groups=mesh['group'=2,'space'=8,'member'=2,'level'=1] {'space','member'}, use_global_device_ids=true, to_apply=%region_6.7 | all-reduce | flops 4096 | bytes 32768 | tf_op jit(solution)/shard_map/psum | solution.py:98
  357.1 0.0 all-to-all-done.2
  357.1 6.4 %copy.38 = bf16[128,8,16,128]{3,0,2,1:T(8,128)(2,1)} copy(bf16[128,8,16,128]{0,3,2,1:T(8,128)(2,1)} %all-to-all-done.2) | data formatting | bytes 8388608 | tf_op jit(solution)/shard_map/all_to_all | solution.py:79
  363.5 4.3 %gather_fusion.1 = bf16[64,128,128]{2,1,0:T(8,128)(2,1)} fusion(bf16[128,128,128]{2,0,1:T(8,128)(2,1)} %bitcast.104, s32[1024]{0:T(1024)S(1)} %pad_clamp_fusion), kind=kCustom, calls=%fused_computation.1 | custom fusion | bytes 4194560 | tf_op jit(solution)/shard_map/jit(_take)/gather | solution.py:80
  367.9 3.3 fusion.11
  371.2 0.0 all-reduce.2.cloned.1.call-done
  371.2 1.9 copy.52
  (7 shorter events, 0.0 us)
Async XLA Ops:
  7.2 10.1 %copy-start = (bf16[16,4,128,128]{3,2,1,0:T(8,128)(2,1)S(1)}, bf16[16,4,128,128]{3,2,1,0:T(8,128)(2,1)}, u32[]{:S(2)}) copy-start(bf16[16,4,128,128]{3,2,1,0:T(8,128)(2,1)} %param.9) | copy-start | bytes 6291460
  11.0 26.5 %all-to-all-start = ((s32[8,1,16]{2,1,0:T(1,128)}), s32[8,1,16]{2,1,0:T(1,128)S(1)}, u32[]{:S(2)}, u32[]{:S(2)}) async-start(s32[8,1,16]{2,1,0:T(1,128)} %bitcast.2), calls=%async_computation | async-start | bytes 8192 | tf_op jit(solution)/shard_map/all_to_all | solution.py:58
  37.5 5.2 %copy-start.6 = (s32[32,128]{1,0:T(8,128)S(1)}, s32[32,128]{1,0:T(8,128)}, u32[]{:S(2)}) copy-start(s32[32,128]{1,0:T(8,128)} %param.12) | copy-start | bytes 49156
  37.5 99.3 %all-to-all-start.1 = ((bf16[8,16,128,128]{3,2,1,0:T(8,128)(2,1)}), bf16[8,16,128,128]{3,2,1,0:T(8,128)(2,1)}, u32[]{:S(2)}, u32[]{:S(2)}) async-start(bf16[8,16,128,128]{3,2,1,0:T(8,128)(2,1)} %bitcast.102), calls=%async_computation.1 | async-start | bytes 8388608 | tf_op jit(solution)/shard_map/all_to_all | solution.py:57
  145.0 28.4 %copy-start.8 = (bf16[128,1024]{1,0:T(8,128)(2,1)S(1)}, bf16[128,1024]{1,0:T(8,128)(2,1)}, u32[]{:S(2)}) copy-start(bf16[128,1024]{1,0:T(8,128)(2,1)} %param.14) | copy-start | bytes 786436
  173.4 8.5 %copy-start.3 = (bf16[33,128,128]{1,2,0:T(8,128)(2,1)}, bf16[33,128,128]{1,2,0:T(8,128)(2,1)S(1)}, u32[]{:S(2)}) copy-start(bf16[33,128,128]{1,2,0:T(8,128)(2,1)S(1)} %copy.36) | copy-start | bytes 3244036
  173.4 8.5 %copy-start.5 = (f32[1,32,4,128]{3,2,1,0:T(4,128)S(1)}, f32[1,32,4,128]{3,2,1,0:T(4,128)}, u32[]{:S(2)}) copy-start(f32[1,32,4,128]{3,2,1,0:T(4,128)} %param.13) | copy-start | bytes 196612
  173.4 8.4 %copy-start.7 = (bf16[1024,4]{0,1:T(4,128)(2,1)S(1)}, bf16[1024,4]{0,1:T(4,128)(2,1)}, u32[]{:S(2)}) copy-start(bf16[1024,4]{0,1:T(4,128)(2,1)} %param.15) | copy-start | bytes 24580
  181.8 3.2 copy-start.1
  200.2 3.2 copy-start.2
  208.8 4.9 %copy-start.4 = (bf16[33,128,128]{1,2,0:T(8,128)(2,1)S(1)}, bf16[33,128,128]{1,2,0:T(8,128)(2,1)}, u32[]{:S(2)}) copy-start(bf16[33,128,128]{1,2,0:T(8,128)(2,1)} %copy-done.3) | copy-start | bytes 3244036
  208.8 148.3 %all-to-all-start.2 = ((bf16[128,8,16,128]{0,3,2,1:T(8,128)(2,1)}), bf16[128,8,16,128]{0,3,2,1:T(8,128)(2,1)}, u32[]{:S(2)}, u32[]{:S(2)}) async-start(bf16[128,8,16,128]{0,3,2,1:T(8,128)(2,1)} %bitcast.103), calls=%async_computation.2 | async-start | bytes 8388608 | tf_op jit(solution)/shard_map/all_to_all | solution.py:79
  213.6 157.6 %all-reduce.2.cloned.1.call-start = ((), (), s32[]{:S(2)}) async-start(), calls=%async_computation.3 | async-start | bytes 1048576 | tf_op jit(solution)/shard_map/psum | solution.py:98
Sparse Core Ops, SparseCore 0:
  219.3 119.8 all-reduce.1
where the time goes:
time: 381 us; the launch traced here: 380 us
  blocking collectives  132 us (35%)
  waiting for transfers between devices  92.8 us (24%)
  matrix products  45.8 us (12%)
  local copies, waits for them, and re-layouts  44.8 us (12%)
  other arithmetic  33.9 us (9%)
  starting transfers between devices  16.3 us (4%)
  between operations  14.2 us (4%)
    psum x1, blocking collectives, body(): grad_in, grad_out = lax.psum((grad_in, grad_out), ('space', 'member'))  132 us
    all_to_all x1, waiting for transfers between devices, body(): lax.all_to_all(outgoing, 'space', split_axis=0, concat_axis=0, tiled=True)  92.7 us
    scatter-add x1, other arithmetic, add_pieces(): summed = summed.at[received_ids.reshape(-1)].add(flat_data)  26.3 us
    dot_general x1, matrix products, body(): jnp.einsum('hq,oqj->ohj', w_out.astype(jnp.float32), misfit, precision=la...  15.1 us
    scatter x1, local copies, waits for them, and re-layouts, remap_pieces(): return jnp.zeros((slot_total, source.shape[1], source.shape[2]), jnp.bflo...  9.99 us
    dot_general x1, matrix products, body(): jnp.einsum('ch,ocj->ohj', w_in, features, preferred_element_type=jnp.floa...  8.42 us
    unnamed x21, local copies, waits for them, and re-layouts  7.75 us
  transfers between devices with their start and end apart: 4, of which 1 were waited for; matrix products, arithmetic and copies ran while one was open for 12% of the time, Pallas kernels for 0%

commit v1 on v0

--- a/solution.py
+++ b/solution.py
@@ -3,6 +3,8 @@
 import jax
 import jax.numpy as jnp
 from jax import lax
+from jax.experimental import pallas as pl
+from jax.experimental.pallas import tpu as pltpu
 from jax.sharding import PartitionSpec as P
 
 
@@ -26,7 +28,7 @@
     return summed[:ocean_blocks].astype(jnp.bfloat16)
 
 
-def body(atm_state, remap_tiles, dest_device, dest_block, wet_mask, target, w_in, w_out):
+def general_body(atm_state, remap_tiles, dest_device, dest_block, wet_mask, target, w_in, w_out):
     space_size = lax.axis_size("space")
     member_size = lax.axis_size("member")
     level_size = lax.axis_size("level")
@@ -99,7 +101,241 @@
     return (adjoint[None], grad_in, grad_out)
 
 
+VMEM_BYTES = 48 * 1024 * 1024
+
+
+def pieces_kernel(slot_ref, state_ref, tiles_ref, out_ref):
+    step = pl.program_id(0)
+    blocks, top_count = tiles_ref.shape[:2]
+    for a in range(blocks):
+        for k in range(top_count):
+            slot = slot_ref[(step * blocks + a) * top_count + k]
+            out_ref[slot] = jnp.dot(
+                state_ref[a], tiles_ref[a, k], preferred_element_type=jnp.float32
+            ).astype(jnp.bfloat16)
+
+
+def slotted_pieces(slot_index, state, tiles, slot_total):
+    atm_blocks, top_count, cells, _ = tiles.shape
+    channels = state.shape[1]
+    per_step = math.gcd(atm_blocks, 4)
+    return pl.pallas_call(
+        pieces_kernel,
+        out_shape=jax.ShapeDtypeStruct((slot_total, channels, cells), jnp.bfloat16),
+        grid_spec=pltpu.PrefetchScalarGridSpec(
+            num_scalar_prefetch=1,
+            grid=(atm_blocks // per_step,),
+            in_specs=[
+                pl.BlockSpec((per_step, channels, cells), lambda s, _: (s, 0, 0)),
+                pl.BlockSpec((per_step, top_count, cells, cells), lambda s, _: (s, 0, 0, 0)),
+            ],
+            out_specs=pl.BlockSpec((slot_total, channels, cells), lambda s, _: (0, 0, 0)),
+        ),
+        compiler_params=pltpu.CompilerParams(vmem_limit_bytes=VMEM_BYTES),
+    )(slot_index, state, tiles)
+
+
+def adjoint_kernel(slot_ref, back_ref, tiles_ref, out_ref):
+    step = pl.program_id(0)
+    blocks, top_count = tiles_ref.shape[:2]
+    for a in range(blocks):
+        first = (step * blocks + a) * top_count
+        grads = jnp.concatenate([back_ref[slot_ref[first + k]] for k in range(top_count)], axis=1)
+        wide = jnp.concatenate([tiles_ref[a, k] for k in range(top_count)], axis=1)
+        out_ref[a] = lax.dot_general(
+            grads, wide, (((1,), (1,)), ((), ())), preferred_element_type=jnp.float32
+        )
+
+
+def adjoint_of(slot_index, returned, tiles):
+    atm_blocks, top_count, cells, _ = tiles.shape
+    slots, channels, _ = returned.shape
+    per_step = math.gcd(atm_blocks, 4)
+    return pl.pallas_call(
+        adjoint_kernel,
+        out_shape=jax.ShapeDtypeStruct((atm_blocks, channels, cells), jnp.float32),
+        grid_spec=pltpu.PrefetchScalarGridSpec(
+            num_scalar_prefetch=1,
+            grid=(atm_blocks // per_step,),
+            in_specs=[
+                pl.BlockSpec((slots, channels, cells), lambda s, _: (0, 0, 0)),
+                pl.BlockSpec((per_step, top_count, cells, cells), lambda s, _: (s, 0, 0, 0)),
+            ],
+            out_specs=pl.BlockSpec((per_step, channels, cells), lambda s, _: (s, 0, 0)),
+        ),
+        compiler_params=pltpu.CompilerParams(vmem_limit_bytes=VMEM_BYTES),
+    )(slot_index, returned, tiles)
+
+
+def network_kernel(
+    scale_in,
+    scale_out,
+    id_ref,
+    received_ref,
+    mask_ref,
+    goal_ref,
+    w_in_ref,
+    w_in_t_ref,
+    w_out_t_ref,
+    w_out_3_ref,
+    reply_ref,
+    grads_ref,
+    total_ref,
+    grad_ref,
+    pre_ref,
+    act_ref,
+    out_ref,
+):
+    slots = received_ref.shape[0]
+    ocean_blocks = goal_ref.shape[0]
+    hidden, channels = w_in_t_ref.shape
+    cells = received_ref.shape[2]
+    group = math.gcd(ocean_blocks, 4)
+    chunk = math.gcd(hidden, 256)
+    total_ref[...] = jnp.zeros_like(total_ref)
+    grads_ref[...] = jnp.zeros_like(grads_ref)
+    out_ref[...] = jnp.zeros_like(out_ref)
+
+    @pl.loop(0, slots)
+    def _(slot):
+        block = id_ref[slot]
+        total_ref[block] += received_ref[slot].astype(jnp.float32)
+
+    @pl.loop(0, ocean_blocks // group)
+    def _(step):
+        first = step * group
+        feat = jnp.concatenate(
+            [total_ref[first + g].astype(jnp.bfloat16) for g in range(group)], axis=1
+        )
+        predicted = jnp.zeros((8, group * cells), jnp.float32)
+        for h in range(0, hidden, chunk):
+            rows = slice(h, h + chunk)
+            pre = jnp.dot(w_in_t_ref[rows], feat, preferred_element_type=jnp.float32)
+            pre_ref[rows] = pre
+            act = (pre * jax.nn.sigmoid(pre)).astype(jnp.bfloat16)
+            act_ref[rows] = act
+            predicted += jnp.dot(w_out_t_ref[:, rows], act, preferred_element_type=jnp.float32)
+        goal = jnp.concatenate([goal_ref[first + g] for g in range(group)], axis=1)
+        mask = jnp.concatenate([mask_ref[first + g] for g in range(group)], axis=1)
+        misfit = mask * (predicted - goal)
+        high = misfit.astype(jnp.bfloat16).astype(jnp.float32)
+        rest = misfit - high
+        middle = rest.astype(jnp.bfloat16).astype(jnp.float32)
+        low = rest - middle
+        misfit_3 = jnp.concatenate([high, middle, low, jnp.zeros_like(low)], axis=0).astype(
+            jnp.bfloat16
+        )
+        feat_grad = jnp.zeros((channels, group * cells), jnp.float32)
+        for h in range(0, hidden, chunk):
+            rows = slice(h, h + chunk)
+            act_grad = jnp.dot(w_out_3_ref[rows], misfit_3, preferred_element_type=jnp.float32)
+            pre = pre_ref[rows]
+            gate = jax.nn.sigmoid(pre)
+            pre_grad = (act_grad * gate * (1.0 + pre * (1.0 - gate))).astype(jnp.bfloat16)
+            feat_grad += jnp.dot(w_in_ref[:, rows], pre_grad, preferred_element_type=jnp.float32)
+            grads_ref[0:channels, rows] += lax.dot_general(
+                feat, pre_grad, (((1,), (1,)), ((), ())), preferred_element_type=jnp.float32
+            )
+            out_ref[:, rows] += lax.dot_general(
+                misfit_3, act_ref[rows], (((1,), (1,)), ((), ())), preferred_element_type=jnp.float32
+            )
+        for g in range(group):
+            grad_ref[first + g] = feat_grad[:, g * cells : (g + 1) * cells].astype(jnp.bfloat16)
+
+    grads_ref[0:channels] = scale_in * grads_ref[0:channels]
+    grads_ref[channels : channels + 8] = scale_out * (out_ref[0:8] + out_ref[8:16] + out_ref[16:24])
+
+    @pl.loop(0, slots)
+    def _(slot):
+        reply_ref[slot] = grad_ref[jnp.minimum(id_ref[slot], ocean_blocks - 1)]
+
+
+def network(received, ids, wet_mask, target, w_in, w_out, scale_in, scale_out):
+    slots, channels, cells = received.shape
+    ocean_blocks, outputs, _ = target.shape
+    hidden = w_in.shape[1]
+    group = math.gcd(ocean_blocks, 4)
+    padded = jnp.pad(w_out, ((0, 0), (0, 8 - outputs)))
+    whole = pl.BlockSpec(memory_space=pltpu.VMEM)
+    return pl.pallas_call(
+        lambda *refs: network_kernel(scale_in, scale_out, *refs),
+        out_shape=(
+            jax.ShapeDtypeStruct((slots, channels, cells), jnp.bfloat16),
+            jax.ShapeDtypeStruct((channels + 8, hidden), jnp.float32),
+        ),
+        in_specs=[pl.BlockSpec(memory_space=pltpu.SMEM)] + [whole] * 7,
+        out_specs=(whole, whole),
+        scratch_shapes=[
+            pltpu.VMEM((ocean_blocks + 1, channels, cells), jnp.float32),
+            pltpu.VMEM((ocean_blocks, channels, cells), jnp.bfloat16),
+            pltpu.VMEM((hidden, group * cells), jnp.float32),
+            pltpu.VMEM((hidden, group * cells), jnp.bfloat16),
+            pltpu.VMEM((32, hidden), jnp.float32),
+        ],
+        compiler_params=pltpu.CompilerParams(vmem_limit_bytes=VMEM_BYTES),
+    )(
+        ids,
+        received,
+        wet_mask.astype(jnp.float32)[:, None, :],
+        jnp.pad(target, ((0, 0), (0, 8 - outputs), (0, 0))),
+        w_in,
+        w_in.T,
+        padded.T,
+        jnp.concatenate([padded, padded, padded, jnp.zeros_like(padded)], axis=1),
+    )
+
+
+def fused_body(atm_state, remap_tiles, dest_device, dest_block, wet_mask, target, w_in, w_out):
+    space_size = lax.axis_size("space")
+    member_size = lax.axis_size("member")
+    atm_blocks, top_count, cells, _ = remap_tiles.shape
+    ocean_blocks = wet_mask.shape[0]
+    channels = atm_state.shape[2]
+    capacity = min(atm_blocks, max(2, 2 * atm_blocks * top_count // space_size))
+    pair_count = atm_blocks * top_count
+    slot_total = space_size * capacity
+    dest_flat = dest_device.reshape(pair_count)
+    onehot = (dest_flat[:, None] == jnp.arange(space_size, dtype=jnp.int32)[None, :]).astype(
+        jnp.int32
+    )
+    slot_rank = jnp.sum((jnp.cumsum(onehot, axis=0) - onehot) * onehot, axis=1)
+    slot_index = dest_flat * capacity + slot_rank
+    send_ids = (
+        jnp.full((slot_total,), ocean_blocks, jnp.int32)
+        .at[slot_index]
+        .set(dest_block.reshape(pair_count))
+    )
+    received_ids = lax.all_to_all(
+        send_ids.reshape(space_size, capacity), "space", split_axis=0, concat_axis=0, tiled=True
+    ).reshape(slot_total)
+    outgoing = slotted_pieces(slot_index, atm_state[0], remap_tiles, slot_total)
+    received = lax.all_to_all(
+        outgoing.reshape(space_size, capacity, channels, cells),
+        "space",
+        split_axis=0,
+        concat_axis=0,
+        tiled=True,
+    ).reshape(slot_total, channels, cells)
+    cell_total = member_size * space_size * ocean_blocks * cells
+    scale_in = math.sqrt(w_in.shape[1] / cell_total)
+    scale_out = 1.0 / math.sqrt(cell_total)
+    reply, grads = network(
+        received, received_ids, wet_mask, target[0], w_in, w_out, scale_in, scale_out
+    )
+    returned = lax.all_to_all(
+        reply.reshape(space_size, capacity, channels, cells),
+        "space",
+        split_axis=0,
+        concat_axis=0,
+        tiled=True,
+    ).reshape(slot_total, channels, cells)
+    grads = lax.psum(grads, ("space", "member"))
+    adjoint = adjoint_of(slot_index, returned, remap_tiles)
+    return (adjoint[None], grads[:channels], grads[channels : channels + w_out.shape[1]].T)
+
+
 def solution(mesh):
+    body = fused_body if mesh.shape["level"] == 1 else general_body
     return jax.shard_map(
         body,
         mesh=mesh,

time: 381 us -> 298 us (0.78)
  blocking collectives: 132 us -> 0 us
  waiting for transfers between devices: 92.8 us -> 218 us
  matrix products: 45.8 us -> 0 us
  Pallas kernels: 0 us -> 34.8 us
  local copies, waits for them, and re-layouts: 44.8 us -> 12.2 us
  other arithmetic: 33.9 us -> 1.79 us
    psum x1 -> x0, blocking collectives: 132 us -> none  [body(): grad_in, grad_out = lax.psum((grad_in, grad_out), ('space', 'member'))]
    psum x1, waiting for transfers between devices: 0.01 us -> 125 us  [fused_body(): grads = lax.psum(grads, ('space', 'member'))]
    dot_general x8 -> x0, matrix products: 45.8 us -> none  [the longest x1 15.1 us: body(): jnp.einsum('hq,oqj->ohj', w_out.astype(jnp.float32), misfit, precision=la...]
    pallas_call x0 -> x3, Pallas kernels: none -> 34.8 us  [the longest x1 26 us: network(): pl.pallas_call(lambda *refs: network_kernel(scale_in, scale_out, *refs),...]
    scatter-add x1 -> x0, other arithmetic: 26.3 us -> none  [add_pieces(): summed = summed.at[received_ids.reshape(-1)].add(flat_data)]
    scatter x2 -> x1, local copies, waits for them, and re-layouts: 10.8 us -> 0.78 us  [fused_body(): send_ids = jnp.full((slot_total,), ocean_blocks, jnp.int32).at[slot_index...]
    gather x2 -> x0, local copies, waits for them, and re-layouts: 7.37 us -> none  [the longest x1 4.33 us: body(): jnp.take(returned.reshape(half_chan, slot_total, cells), slot_index, axis=1)]
    convert_element_type x3 -> x2, other arithmetic: 6.56 us -> 0.08 us  [the longest x1 0.07 us: fused_body(): (dest_flat[:, None] == jnp.arange(space_size, dtype=jnp.int32)[None, :])....]
  transfers between devices with their start and end apart: 4 -> 4, of which waited for: 1 -> 2; matrix products, arithmetic and copies ran while one was open for 12% -> 2% of each run, Pallas kernels for 0% -> 1%
where the time goes in v1:
time: 298 us; the launch traced here: 297 us
  waiting for transfers between devices  218 us (73%)
  Pallas kernels  34.8 us (12%)
  starting transfers between devices  16.3 us (5%)
  between operations  14.2 us (5%)
  local copies, waits for them, and re-layouts  12.2 us (4%)
    psum x1, waiting for transfers between devices, fused_body(): grads = lax.psum(grads, ('space', 'member'))  125 us
    all_to_all x1, waiting for transfers between devices, fused_body(): lax.all_to_all(outgoing.reshape(space_size, capacity, channels, cells), '...  92.3 us
    pallas_call x1, Pallas kernels, network(): pl.pallas_call(lambda *refs: network_kernel(scale_in, scale_out, *refs),...  26 us
    all_to_all x1, starting transfers between devices, fused_body(): lax.all_to_all(send_ids.reshape(space_size, capacity), 'space', split_axi...  6.33 us
    unnamed x19, local copies, waits for them, and re-layouts  6.31 us
  transfers between devices with their start and end apart: 4, of which 2 were waited for; matrix products, arithmetic and copies ran while one was open for 2% of the time, Pallas kernels for 1%

profile of v1, /device:TPU:0, one launch (start us, length us, event | category | flops | bytes accessed | tf_op | source)
XLA Modules:
  0.0 297.2 jit_solution(2771705013183057662)
XLA Ops:
  7.2 0.7 broadcast_multiply_fusion
  7.8 0.8 copy.23
  8.6 0.1 copy.24
  8.7 0.1 mul.28
  8.8 0.8 copy.25
  9.5 0.1 reshape.72
  9.6 0.1 reshape.61
  9.7 0.1 fusion
  9.8 0.1 reduce_window_sum.11
  9.9 0.2 select_reduce_fusion
  10.1 0.8 scatter_custom_fusion
  10.9 0.7 all_to_all.12
  11.6 6.3 %all-to-all-start = ((s32[8,1,16]{2,1,0:T(1,128)}), s32[8,1,16]{2,1,0:T(1,128)S(1)}, u32[]{:S(2)}, u32[]{:S(2)}) async-start(s32[8,1,16]{2,1,0:T(1,128)} %bitcast.2), calls=%async_computation | async-start | bytes 8192 | tf_op jit(solution)/shard_map/all_to_all | solution.py:308
  17.9 0.0 copy-start
  17.9 1.6 copy-done
  19.5 0.0 copy-start.4
  19.5 1.0 copy-done.4
  20.5 3.7 %shard_map.103 = bf16[128,128,128]{2,1,0:T(8,128)(2,1)} custom-call(s32[64]{0:T(128)S(1)} %multiply_add_fusion.slot_ref, bf16[16,128,128]{2,1,0:T(8,128)(2,1)S(1)} %bitcast.23, bf16[16,4,128,128]{3,2,1,0:T(8,128)(2,1)S(1)} %copy-done), custom_call_target="tpu_custom_call" | custom-call | tf_op jit(solution)/shard_map/pallas_call | solution.py:122
  24.3 0.0 all-to-all-done
  24.3 0.0 copy-start.6
  24.3 0.0 copy-start.7
  24.3 0.0 copy-start.3
  24.3 0.0 copy-start.5
  24.3 5.2 %all-to-all-start.1 = ((bf16[8,16,128,128]{3,2,1,0:T(8,128)(2,1)}), bf16[8,16,128,128]{3,2,1,0:T(8,128)(2,1)}, u32[]{:S(2)}, u32[]{:S(2)}) async-start(bf16[8,16,128,128]{3,2,1,0:T(8,128)(2,1)} %bitcast.25), calls=%async_computation.1 | async-start | bytes 8388608 | tf_op jit(solution)/shard_map/all_to_all | solution.py:312
  29.5 0.0 copy-done.6
  29.6 0.1 pad.13.clone
  29.6 0.0 copy-done.7
  29.6 0.1 maximum_maximum_fusion
  29.7 0.2 copy.28.refs_7_
  29.9 0.0 copy-done.3
  29.9 0.2 copy.27
  30.1 0.0 copy-done.5
  30.1 0.5 broadcast.37
  30.6 0.7 reduce.3
  31.3 0.1 reshape.63.refs_0_
  31.4 92.3 %all-to-all-done.1 = bf16[8,16,128,128]{3,2,1,0:T(8,128)(2,1)} async-done(((bf16[8,16,128,128]{3,2,1,0:T(8,128)(2,1)}), bf16[8,16,128,128]{3,2,1,0:T(8,128)(2,1)}, u32[]{:S(2)}, u32[]{:S(2)}) %all-to-all-start.1) | async-done | bytes 4194336 | tf_op jit(solution)/shard_map/all_to_all | solution.py:312
  123.6 26.0 %shard_map.104 = (bf16[128,128,128]{2,1,0:T(8,128)(2,1)S(1)}, f32[136,1024]{1,0:T(8,128)}) custom-call(s32[128]{0:T(128)S(1)} %reshape.63.refs_0_, bf16[128,128,128]{2,1,0:T(8,128)(2,1)} %bitcast.5.refs_1_, f32[32,1,128]{2,1,0:T(1,128)S(1)} %bitcast.24, f32[32,8,128]{2,1,0:T(8,128)S(1)} %pad.8.refs_3_, bf16[128,1024]{1,0:T(8,128)(2,1)S(1)} %copy-done.3, ...), custom_call_target="tpu_custom_call" | custom-call | tf_op jit(solution)/shard_map/pallas_call | solution.py:260
  149.6 0.0 copy-start.2
  149.6 2.0 copy-done.2
  151.6 0.0 copy-start.1
  151.6 4.7 %all-to-all-start.2 = ((bf16[8,16,128,128]{3,2,1,0:T(8,128)(2,1)}), bf16[8,16,128,128]{3,2,1,0:T(8,128)(2,1)}, u32[]{:S(2)}, u32[]{:S(2)}) async-start(bf16[8,16,128,128]{3,2,1,0:T(8,128)(2,1)} %bitcast.21), calls=%async_computation.2 | async-start | bytes 8388608 | tf_op jit(solution)/shard_map/all_to_all | solution.py:325
  156.3 0.0 all-reduce.4.cloned.1.call-start
  156.3 0.7 all-reduce.4.cloned.1.call-update
  157.0 125.0 %all-reduce.4.cloned.1.call-done = f32[136,1024]{1,0:T(8,128)} async-done(((f32[136,1024]{1,0:T(8,128)}), f32[136,1024]{1,0:T(8,128)}) %all-reduce.4.cloned.1.call-update) | async-done | bytes 557072 | tf_op jit(solution)/shard_map/psum | solution.py:332
  282.0 1.9 slice.8
  283.9 1.4 slice_bitcast_fusion
  285.3 0.0 all-to-all-done.2
  285.3 0.0 copy-done.1
  285.3 5.1 %shard_map.105 = f32[16,128,128]{2,1,0:T(8,128)} custom-call(s32[64]{0:T(128)S(1)} %multiply_add_fusion.slot_ref, bf16[128,128,128]{2,1,0:T(8,128)(2,1)} %bitcast.11.back_ref, bf16[16,4,128,128]{3,2,1,0:T(8,128)(2,1)S(1)} %copy-done.1), custom_call_target="tpu_custom_call" | custom-call | tf_op jit(solution)/shard_map/pallas_call | solution.py:154
  (6 shorter events, 0.0 us)
Async XLA Ops:
  11.6 12.7 %all-to-all-start = ((s32[8,1,16]{2,1,0:T(1,128)}), s32[8,1,16]{2,1,0:T(1,128)S(1)}, u32[]{:S(2)}, u32[]{:S(2)}) async-start(s32[8,1,16]{2,1,0:T(1,128)} %bitcast.2), calls=%async_computation | async-start | bytes 8192 | tf_op jit(solution)/shard_map/all_to_all | solution.py:308
  17.9 1.6 copy-start
  19.5 1.0 copy-start.4
  24.3 5.3 %copy-start.6 = (s32[32,128]{1,0:T(8,128)S(1)}, s32[32,128]{1,0:T(8,128)}, u32[]{:S(2)}) copy-start(s32[32,128]{1,0:T(8,128)} %param.12) | copy-start | bytes 49156
  24.3 5.4 %copy-start.7 = (bf16[1024,4]{0,1:T(4,128)(2,1)S(1)}, bf16[1024,4]{0,1:T(4,128)(2,1)}, u32[]{:S(2)}) copy-start(bf16[1024,4]{0,1:T(4,128)(2,1)} %param.15) | copy-start | bytes 24580
  24.3 5.6 %copy-start.3 = (bf16[128,1024]{1,0:T(8,128)(2,1)S(1)}, bf16[128,1024]{1,0:T(8,128)(2,1)}, u32[]{:S(2)}) copy-start(bf16[128,1024]{1,0:T(8,128)(2,1)} %refs_4_.1) | copy-start | bytes 786436
  24.3 5.8 %copy-start.5 = (f32[1,32,4,128]{3,2,1,0:T(4,128)S(1)}, f32[1,32,4,128]{3,2,1,0:T(4,128)}, u32[]{:S(2)}) copy-start(f32[1,32,4,128]{3,2,1,0:T(4,128)} %param.13) | copy-start | bytes 196612
  24.3 99.3 %all-to-all-start.1 = ((bf16[8,16,128,128]{3,2,1,0:T(8,128)(2,1)}), bf16[8,16,128,128]{3,2,1,0:T(8,128)(2,1)}, u32[]{:S(2)}, u32[]{:S(2)}) async-start(bf16[8,16,128,128]{3,2,1,0:T(8,128)(2,1)} %bitcast.25), calls=%async_computation.1 | async-start | bytes 8388608 | tf_op jit(solution)/shard_map/all_to_all | solution.py:312
  149.6 2.0 copy-start.2
  151.6 133.7 %copy-start.1 = (bf16[16,4,128,128]{3,2,1,0:T(8,128)(2,1)S(1)}, bf16[16,4,128,128]{3,2,1,0:T(8,128)(2,1)}, u32[]{:S(2)}) copy-start(bf16[16,4,128,128]{3,2,1,0:T(8,128)(2,1)} %tiles_ref.3) | copy-start | bytes 6291460
  151.6 133.7 %all-to-all-start.2 = ((bf16[8,16,128,128]{3,2,1,0:T(8,128)(2,1)}), bf16[8,16,128,128]{3,2,1,0:T(8,128)(2,1)}, u32[]{:S(2)}, u32[]{:S(2)}) async-start(bf16[8,16,128,128]{3,2,1,0:T(8,128)(2,1)} %bitcast.21), calls=%async_computation.2 | async-start | bytes 8388608 | tf_op jit(solution)/shard_map/all_to_all | solution.py:325
  156.3 125.8 %all-reduce.4.cloned.1.call-start = ((), (), s32[]{:S(2)}) async-start(), calls=%async_computation.3 | async-start | bytes 1114112 | tf_op jit(solution)/shard_map/psum | solution.py:332
Sparse Core Ops, SparseCore 0:
  161.1 120.8 all-reduce.3

commit v2 on v1

--- a/solution.py
+++ b/solution.py
@@ -178,10 +178,10 @@
     w_in_t_ref,
     w_out_t_ref,
     w_out_3_ref,
-    reply_ref,
+    grad_ref,
+    pieces_ref,
+    total_ref,
     grads_ref,
-    total_ref,
-    grad_ref,
     pre_ref,
     act_ref,
     out_ref,
@@ -233,7 +233,7 @@
             gate = jax.nn.sigmoid(pre)
             pre_grad = (act_grad * gate * (1.0 + pre * (1.0 - gate))).astype(jnp.bfloat16)
             feat_grad += jnp.dot(w_in_ref[:, rows], pre_grad, preferred_element_type=jnp.float32)
-            grads_ref[0:channels, rows] += lax.dot_general(
+            grads_ref[:, rows] += lax.dot_general(
                 feat, pre_grad, (((1,), (1,)), ((), ())), preferred_element_type=jnp.float32
             )
             out_ref[:, rows] += lax.dot_general(
@@ -242,12 +242,13 @@
         for g in range(group):
             grad_ref[first + g] = feat_grad[:, g * cells : (g + 1) * cells].astype(jnp.bfloat16)
 
-    grads_ref[0:channels] = scale_in * grads_ref[0:channels]
-    grads_ref[channels : channels + 8] = scale_out * (out_ref[0:8] + out_ref[8:16] + out_ref[16:24])
-
-    @pl.loop(0, slots)
-    def _(slot):
-        reply_ref[slot] = grad_ref[jnp.minimum(id_ref[slot], ocean_blocks - 1)]
+    out = scale_out * (out_ref[0:8] + out_ref[8:16] + out_ref[16:24])
+    for p in range(pieces_ref.shape[0]):
+        pieces_ref[p, :, 0:hidden] = scale_in * grads_ref[8 * p : 8 * p + 8]
+        if (p + 1) * 128 <= hidden:
+            pieces_ref[p, :, hidden : hidden + 128] = out[:, p * 128 : (p + 1) * 128]
+        else:
+            pieces_ref[p, :, hidden : hidden + 128] = jnp.zeros((8, 128), jnp.float32)
 
 
 def network(received, ids, wet_mask, target, w_in, w_out, scale_in, scale_out):
@@ -260,14 +261,14 @@
     return pl.pallas_call(
         lambda *refs: network_kernel(scale_in, scale_out, *refs),
         out_shape=(
-            jax.ShapeDtypeStruct((slots, channels, cells), jnp.bfloat16),
-            jax.ShapeDtypeStruct((channels + 8, hidden), jnp.float32),
+            jax.ShapeDtypeStruct((ocean_blocks, channels, cells), jnp.bfloat16),
+            jax.ShapeDtypeStruct((channels // 8, 8, hidden + 128), jnp.float32),
         ),
         in_specs=[pl.BlockSpec(memory_space=pltpu.SMEM)] + [whole] * 7,
         out_specs=(whole, whole),
         scratch_shapes=[
             pltpu.VMEM((ocean_blocks + 1, channels, cells), jnp.float32),
-            pltpu.VMEM((ocean_blocks, channels, cells), jnp.bfloat16),
+            pltpu.VMEM((channels, hidden), jnp.float32),
             pltpu.VMEM((hidden, group * cells), jnp.float32),
             pltpu.VMEM((hidden, group * cells), jnp.bfloat16),
             pltpu.VMEM((32, hidden), jnp.float32),
@@ -285,12 +286,214 @@
     )
 
 
+CHUNKS = 2
+MESH = pl.DeviceIdType.MESH
+
+
+def exchange_kernel(
+    space_size,
+    member_size,
+    feat_ref,
+    grads_ref,
+    all_ref,
+    sums_ref,
+    inbox,
+    total,
+    term_send,
+    term_recv,
+    sum_send,
+    sum_recv,
+    line_send,
+    line_recv,
+    pair_send,
+    pair_recv,
+    own_sem,
+):
+    space, member = lax.axis_index("space"), lax.axis_index("member")
+    ranks = space_size * member_size
+    rank = member * space_size + space
+    length = space_size // 2
+    place, core = space // 2, space % 2
+    size = feat_ref.shape[0] // CHUNKS
+
+    def peer(i):
+        other = lax.rem(rank + i, ranks)
+        return other, {"space": other % space_size, "member": other // space_size}
+
+    barrier = pltpu.get_barrier_semaphore()
+    for i in range(1, ranks):
+        pl.semaphore_signal(barrier, inc=1, device_id=peer(i)[1], device_id_type=MESH)
+    pl.semaphore_wait(barrier, ranks - 1)
+
+    def term(i):
+        other, device = peer(i)
+        return pltpu.make_async_remote_copy(
+            src_ref=grads_ref.at[other],
+            dst_ref=inbox.at[i - 1],
+            send_sem=term_send.at[i - 1],
+            recv_sem=term_recv.at[i - 1],
+            device_id=device,
+            device_id_type=MESH,
+        )
+
+    def piece(i, owner):
+        return pltpu.make_async_remote_copy(
+            src_ref=total,
+            dst_ref=sums_ref.at[owner],
+            send_sem=sum_send.at[i - 1],
+            recv_sem=sum_recv.at[i - 1],
+            device_id=peer(i)[1],
+            device_id_type=MESH,
+        )
+
+    def source(origin, own, c):
+        rows = pl.ds(c * size, size)
+        return feat_ref.at[rows] if own else all_ref.at[origin, rows]
+
+    def line(way, hop, c, origin, own):
+        step = 1 if way == 0 else -1
+        return pltpu.make_async_remote_copy(
+            src_ref=source(origin, own, c),
+            dst_ref=all_ref.at[origin, pl.ds(c * size, size)],
+            send_sem=line_send.at[way, hop, c],
+            recv_sem=line_recv.at[way, hop, c],
+            device_id={"space": (place + step) * 2 + core},
+            device_id_type=MESH,
+        )
+
+    def pair(index, c, origin, own):
+        return pltpu.make_async_remote_copy(
+            src_ref=source(origin, own, c),
+            dst_ref=all_ref.at[origin, pl.ds(c * size, size)],
+            send_sem=pair_send.at[index, c],
+            recv_sem=pair_recv.at[index, c],
+            device_id={"space": place * 2 + 1 - core},
+            device_id_type=MESH,
+        )
+
+    def behind(way, hop):
+        at = place - 1 - hop if way == 0 else place + 1 + hop
+        return at, (at >= 0 if way == 0 else at < length)
+
+    ahead = (place < length - 1, place > 0)
+    own_copy = pltpu.make_async_copy(feat_ref, all_ref.at[space], own_sem.at[0])
+    for c in range(CHUNKS):
+        for way in range(2):
+
+            @pl.when(ahead[way])
+            def _():
+                line(way, 0, c, space, True).start()
+
+    for i in range(1, ranks):
+        term(i).start()
+    for c in range(CHUNKS):
+        pair(0, c, space, True).start()
+    own_copy.start()
+
+    for hop in range(length - 1):
+        for c in range(CHUNKS):
+            for way in range(2):
+                at, there = behind(way, hop)
+                origin = at * 2 + core
+
+                @pl.when(there)
+                def _():
+                    line(way, hop, c, origin, False).wait_recv()
+                    if hop + 1 < length - 1:
+
+                        @pl.when(ahead[way])
+                        def _():
+                            line(way, hop + 1, c, origin, False).start()
+
+                    pair(1 + way * (length - 1) + hop, c, origin, False).start()
+
+        if hop == 0:
+            for i in range(1, ranks):
+                term(i).wait_recv()
+            value = grads_ref[rank]
+            for i in range(1, ranks):
+                value += inbox[i - 1]
+            total[...] = value
+            for i in range(1, ranks):
+                piece(i, rank).start()
+            own_sum = pltpu.make_async_copy(total, sums_ref.at[rank], own_sem.at[1])
+            own_sum.start()
+
+    own_copy.wait()
+    own_sum.wait()
+    for i in range(1, ranks):
+        piece(i, lax.rem(rank + ranks - i, ranks)).wait_recv()
+        piece(i, rank).wait_send()
+        term(i).wait_send()
+    for c in range(CHUNKS):
+        pair(0, c, space, True).wait_send()
+        pair(0, c, place * 2 + 1 - core, False).wait_recv()
+        for way in range(2):
+
+            @pl.when(ahead[way])
+            def _():
+                line(way, 0, c, space, True).wait_send()
+
+            for hop in range(length - 1):
+                at, there = behind(way, hop)
+                origin = at * 2 + core
+                index = 1 + way * (length - 1) + hop
+
+                @pl.when(there)
+                def _():
+                    if hop + 1 < length - 1:
+
+                        @pl.when(ahead[way])
+                        def _():
+                            line(way, hop + 1, c, origin, False).wait_send()
+
+                    pair(index, c, origin, False).wait_send()
+                    pair(index, c, at * 2 + 1 - core, False).wait_recv()
+
+
+def exchange(feat_grad, grads, space_size, member_size):
+    peers = space_size * member_size - 1
+    hops = max(1, space_size // 2 - 1)
+    dma = pltpu.SemaphoreType.DMA
+    anywhere = pl.BlockSpec(memory_space=pl.ANY)
+    return pl.pallas_call(
+        lambda *refs: exchange_kernel(space_size, member_size, *refs),
+        out_shape=(
+            jax.ShapeDtypeStruct((space_size,) + feat_grad.shape, feat_grad.dtype),
+            jax.ShapeDtypeStruct(grads.shape, grads.dtype),
+        ),
+        in_specs=[anywhere, pl.BlockSpec(memory_space=pltpu.VMEM)],
+        out_specs=(anywhere, anywhere),
+        scratch_shapes=[
+            pltpu.VMEM((peers,) + grads.shape[1:], grads.dtype),
+            pltpu.VMEM(grads.shape[1:], grads.dtype),
+            dma((peers,)),
+            dma((peers,)),
+            dma((peers,)),
+            dma((peers,)),
+            dma((2, hops, CHUNKS)),
+            dma((2, hops, CHUNKS)),
+            dma((1 + 2 * hops, CHUNKS)),
+            dma((1 + 2 * hops, CHUNKS)),
+            dma((2,)),
+        ],
+        compiler_params=pltpu.CompilerParams(
+            collective_id=0, has_side_effects=True, vmem_limit_bytes=VMEM_BYTES
+        ),
+    )(feat_grad, grads)
+
+
 def fused_body(atm_state, remap_tiles, dest_device, dest_block, wet_mask, target, w_in, w_out):
     space_size = lax.axis_size("space")
     member_size = lax.axis_size("member")
     atm_blocks, top_count, cells, _ = remap_tiles.shape
     ocean_blocks = wet_mask.shape[0]
     channels = atm_state.shape[2]
+    pieces_fit = channels == 8 * space_size * member_size and w_in.shape[1] <= 16 * channels
+    if not pieces_fit or ocean_blocks % CHUNKS:
+        return general_body(
+            atm_state, remap_tiles, dest_device, dest_block, wet_mask, target, w_in, w_out
+        )
     capacity = min(atm_blocks, max(2, 2 * atm_blocks * top_count // space_size))
     pair_count = atm_blocks * top_count
     slot_total = space_size * capacity
@@ -319,23 +522,22 @@
     cell_total = member_size * space_size * ocean_blocks * cells
     scale_in = math.sqrt(w_in.shape[1] / cell_total)
     scale_out = 1.0 / math.sqrt(cell_total)
-    reply, grads = network(
+    feat_grad, grads = network(
         received, received_ids, wet_mask, target[0], w_in, w_out, scale_in, scale_out
     )
-    returned = lax.all_to_all(
-        reply.reshape(space_size, capacity, channels, cells),
-        "space",
-        split_axis=0,
-        concat_axis=0,
-        tiled=True,
-    ).reshape(slot_total, channels, cells)
-    grads = lax.psum(grads, ("space", "member"))
-    adjoint = adjoint_of(slot_index, returned, remap_tiles)
-    return (adjoint[None], grads[:channels], grads[channels : channels + w_out.shape[1]].T)
+    gathered, summed = exchange(feat_grad, grads, space_size, member_size)
+    owner = dest_flat * ocean_blocks + dest_block.reshape(pair_count)
+    adjoint = adjoint_of(
+        owner, gathered.reshape(space_size * ocean_blocks, channels, cells), remap_tiles
+    )
+    hidden, outputs = w_out.shape
+    grad_in = summed[:, :, :hidden].reshape(channels, hidden)
+    grad_out = summed[: hidden // 128, :outputs, hidden:]
+    return (adjoint[None], grad_in, grad_out.transpose(0, 2, 1).reshape(hidden, outputs))
 
 
 def solution(mesh):
-    body = fused_body if mesh.shape["level"] == 1 else general_body
+    body = fused_body if mesh.shape["level"] == 1 and mesh.shape["space"] % 2 == 0 else general_body
     return jax.shard_map(
         body,
         mesh=mesh,

time: 298 us -> 243 us (0.82)
  waiting for transfers between devices: 218 us -> 92.2 us
  Pallas kernels: 34.8 us -> 128 us
  between operations: 14.2 us -> 0.78 us
  starting transfers between devices: 16.3 us -> 11.6 us
  local copies, waits for them, and re-layouts: 12.2 us -> 8.46 us
    psum x1 -> x0, waiting for transfers between devices: 125 us -> none  [fused_body(): grads = lax.psum(grads, ('space', 'member'))]
    pallas_call x0 -> x1, Pallas kernels: none -> 93.5 us  [exchange(): pl.pallas_call(lambda *refs: exchange_kernel(space_size, member_size, *re...]
    all_to_all x1 -> x0, starting transfers between devices: 4.67 us -> none  [fused_body(): lax.all_to_all(reply.reshape(space_size, capacity, channels, cells), 'spa...]
    unnamed x19 -> x17, local copies, waits for them, and re-layouts: 6.31 us -> 4.35 us
  transfers between devices with their start and end apart: 4 -> 2, of which waited for: 2 -> 1; matrix products, arithmetic and copies ran while one was open for 2% -> 1% of each run, Pallas kernels for 1% -> 2%
where the time goes in v2:
time: 243 us; the launch traced here: 242 us
  Pallas kernels  128 us (53%)
  waiting for transfers between devices  92.2 us (38%)
  starting transfers between devices  11.6 us (5%)
  local copies, waits for them, and re-layouts  8.46 us (3%)
    pallas_call x1, Pallas kernels, exchange(): pl.pallas_call(lambda *refs: exchange_kernel(space_size, member_size, *re...  93.5 us
    all_to_all x1, waiting for transfers between devices, fused_body(): lax.all_to_all(outgoing.reshape(space_size, capacity, channels, cells), '...  92.2 us
    pallas_call x1, Pallas kernels, network(): pl.pallas_call(lambda *refs: network_kernel(scale_in, scale_out, *refs),...  24.1 us
    all_to_all x1, starting transfers between devices, fused_body(): lax.all_to_all(send_ids.reshape(space_size, capacity), 'space', split_axi...  6.33 us
    pallas_call x1, Pallas kernels, adjoint_of(): pl.pallas_call(adjoint_kernel, out_shape=jax.ShapeDtypeStruct((atm_blocks...  6.29 us
    all_to_all x1, starting transfers between devices, fused_body(): lax.all_to_all(outgoing.reshape(space_size, capacity, channels, cells), '...  5.24 us
  transfers between devices with their start and end apart: 2, of which 1 were waited for; matrix products, arithmetic and copies ran while one was open for 1% of the time, Pallas kernels for 2%

profile of v2, /device:TPU:0, one launch (start us, length us, event | category | flops | bytes accessed | tf_op | source)
XLA Modules:
  0.0 242.5 jit_solution(9735639305973012607)
XLA Ops:
  0.6 0.7 broadcast_multiply_fusion
  1.3 0.8 copy.23
  2.1 0.1 copy.25
  2.2 0.1 mul.33
  2.2 0.8 copy.24
  3.0 0.1 reshape.77
  3.1 0.1 reshape.65
  3.2 0.1 fusion
  3.3 0.1 reduce_window_sum.11
  3.4 0.2 select_reduce_fusion
  3.6 0.8 scatter_custom_fusion
  4.3 0.7 all_to_all.9
  5.0 6.3 %all-to-all-start = ((s32[8,1,16]{2,1,0:T(1,128)}), s32[8,1,16]{2,1,0:T(1,128)S(1)}, u32[]{:S(2)}, u32[]{:S(2)}) async-start(s32[8,1,16]{2,1,0:T(1,128)} %bitcast.2), calls=%async_computation | async-start | bytes 8192 | tf_op jit(solution)/shard_map/all_to_all | solution.py:511
  11.4 0.0 copy-start
  11.4 1.6 copy-done
  12.9 0.0 copy-start.3
  12.9 1.0 copy-done.3
  14.0 3.7 %shard_map.103 = bf16[128,128,128]{2,1,0:T(8,128)(2,1)} custom-call(s32[64]{0:T(128)S(1)} %get-tuple-element.13.slot_ref, bf16[16,128,128]{2,1,0:T(8,128)(2,1)S(1)} %bitcast.25, bf16[16,4,128,128]{3,2,1,0:T(8,128)(2,1)S(1)} %copy-done), custom_call_target="tpu_custom_call" | custom-call | tf_op jit(solution)/shard_map/pallas_call | solution.py:122
  17.7 0.0 all-to-all-done
  17.7 0.0 copy-start.5
  17.7 0.0 copy-start.6
  17.7 0.0 copy-start.2
  17.7 0.0 copy-start.4
  17.7 5.2 %all-to-all-start.1 = ((bf16[8,16,128,128]{3,2,1,0:T(8,128)(2,1)}), bf16[8,16,128,128]{3,2,1,0:T(8,128)(2,1)}, u32[]{:S(2)}, u32[]{:S(2)}) async-start(bf16[8,16,128,128]{3,2,1,0:T(8,128)(2,1)} %bitcast.27), calls=%async_computation.1 | async-start | bytes 8388608 | tf_op jit(solution)/shard_map/all_to_all | solution.py:515
  23.0 0.0 copy-done.5
  23.0 0.1 pad.13.clone
  23.1 0.0 copy-done.6
  23.1 0.1 maximum_maximum_fusion
  23.2 0.2 copy.28.refs_7_
  23.4 0.0 copy-done.2
  23.4 0.0 copy-start.1
  23.4 0.2 copy.27
  23.6 0.0 copy-done.4
  23.6 0.5 broadcast.37
  24.1 0.7 reduce.3
  24.8 0.1 reshape.67.refs_0_
  24.9 92.2 %all-to-all-done.1 = bf16[8,16,128,128]{3,2,1,0:T(8,128)(2,1)} async-done(((bf16[8,16,128,128]{3,2,1,0:T(8,128)(2,1)}), bf16[8,16,128,128]{3,2,1,0:T(8,128)(2,1)}, u32[]{:S(2)}, u32[]{:S(2)}) %all-to-all-start.1) | async-done | bytes 4194336 | tf_op jit(solution)/shard_map/all_to_all | solution.py:515
  117.1 24.1 %shard_map.104 = (bf16[32,128,128]{2,1,0:T(8,128)(2,1)S(1)}, f32[16,8,1152]{2,1,0:T(8,128)S(1)}) custom-call(s32[128]{0:T(128)S(1)} %reshape.67.refs_0_, bf16[128,128,128]{2,1,0:T(8,128)(2,1)} %bitcast.5.refs_1_, f32[32,1,128]{2,1,0:T(1,128)S(1)} %bitcast.26, f32[32,8,128]{2,1,0:T(8,128)S(1)} %pad.8.refs_3_, bf16[128,1024]{1,0:T(8,128)(2,1)S(1)} %copy-done.2, ...), custom_call_target="tpu_custom_call" | custom-call | tf_op jit(solution)/shard_map/pallas_call | solution.py:261
  141.2 93.5 %shard_map.105 = (bf16[8,32,128,128]{3,2,1,0:T(8,128)(2,1)}, f32[16,8,1152]{2,1,0:T(8,128)S(1)}) custom-call(bf16[32,128,128]{2,1,0:T(8,128)(2,1)S(1)} %get-tuple-element.7.refs_0_, f32[16,8,1152]{2,1,0:T(8,128)S(1)} %get-tuple-element.8.refs_1_), custom_call_target="tpu_custom_call" | custom-call | tf_op jit(solution)/shard_map/pallas_call | solution.py:459
  234.7 0.6 slice_bitcast_fusion.1
  235.3 0.8 slice_bitcast_fusion
  236.2 0.0 copy-done.1
  236.2 6.3 %shard_map.106 = f32[16,128,128]{2,1,0:T(8,128)} custom-call(s32[64]{0:T(128)S(1)} %get-tuple-element.14.slot_ref, bf16[256,128,128]{2,1,0:T(8,128)(2,1)} %bitcast.28, bf16[16,4,128,128]{3,2,1,0:T(8,128)(2,1)S(1)} %copy-done.1), custom_call_target="tpu_custom_call" | custom-call | tf_op jit(solution)/shard_map/pallas_call | solution.py:154
  (6 shorter events, 0.0 us)
Async XLA Ops:
  5.0 12.7 %all-to-all-start = ((s32[8,1,16]{2,1,0:T(1,128)}), s32[8,1,16]{2,1,0:T(1,128)S(1)}, u32[]{:S(2)}, u32[]{:S(2)}) async-start(s32[8,1,16]{2,1,0:T(1,128)} %bitcast.2), calls=%async_computation | async-start | bytes 8192 | tf_op jit(solution)/shard_map/all_to_all | solution.py:511
  11.4 1.6 copy-start
  12.9 1.0 copy-start.3
  17.7 5.3 %copy-start.5 = (s32[32,128]{1,0:T(8,128)S(1)}, s32[32,128]{1,0:T(8,128)}, u32[]{:S(2)}) copy-start(s32[32,128]{1,0:T(8,128)} %param.12) | copy-start | bytes 49156
  17.7 5.4 %copy-start.6 = (bf16[1024,4]{0,1:T(4,128)(2,1)S(1)}, bf16[1024,4]{0,1:T(4,128)(2,1)}, u32[]{:S(2)}) copy-start(bf16[1024,4]{0,1:T(4,128)(2,1)} %param.15) | copy-start | bytes 24580
  17.7 5.6 %copy-start.2 = (bf16[128,1024]{1,0:T(8,128)(2,1)S(1)}, bf16[128,1024]{1,0:T(8,128)(2,1)}, u32[]{:S(2)}) copy-start(bf16[128,1024]{1,0:T(8,128)(2,1)} %refs_4_.1) | copy-start | bytes 786436
  17.7 5.8 %copy-start.4 = (f32[1,32,4,128]{3,2,1,0:T(4,128)S(1)}, f32[1,32,4,128]{3,2,1,0:T(4,128)}, u32[]{:S(2)}) copy-start(f32[1,32,4,128]{3,2,1,0:T(4,128)} %param.13) | copy-start | bytes 196612
  17.7 99.3 %all-to-all-start.1 = ((bf16[8,16,128,128]{3,2,1,0:T(8,128)(2,1)}), bf16[8,16,128,128]{3,2,1,0:T(8,128)(2,1)}, u32[]{:S(2)}, u32[]{:S(2)}) async-start(bf16[8,16,128,128]{3,2,1,0:T(8,128)(2,1)} %bitcast.27), calls=%async_computation.1 | async-start | bytes 8388608 | tf_op jit(solution)/shard_map/all_to_all | solution.py:515
  23.4 212.8 %copy-start.1 = (bf16[16,4,128,128]{3,2,1,0:T(8,128)(2,1)S(1)}, bf16[16,4,128,128]{3,2,1,0:T(8,128)(2,1)}, u32[]{:S(2)}) copy-start(bf16[16,4,128,128]{3,2,1,0:T(8,128)(2,1)} %tiles_ref.3) | copy-start | bytes 6291460

commit v3 on v2

--- a/solution.py
+++ b/solution.py
@@ -104,35 +104,21 @@
 VMEM_BYTES = 48 * 1024 * 1024
 
 
-def pieces_kernel(slot_ref, state_ref, tiles_ref, out_ref):
-    step = pl.program_id(0)
-    blocks, top_count = tiles_ref.shape[:2]
-    for a in range(blocks):
-        for k in range(top_count):
-            slot = slot_ref[(step * blocks + a) * top_count + k]
-            out_ref[slot] = jnp.dot(
-                state_ref[a], tiles_ref[a, k], preferred_element_type=jnp.float32
-            ).astype(jnp.bfloat16)
-
-
-def slotted_pieces(slot_index, state, tiles, slot_total):
-    atm_blocks, top_count, cells, _ = tiles.shape
-    channels = state.shape[1]
-    per_step = math.gcd(atm_blocks, 4)
+def slots_kernel(pair_ref, tiles_ref, out_ref):
+    @pl.loop(0, out_ref.shape[0], unroll=4)
+    def _(slot):
+        out_ref[slot] = tiles_ref[pair_ref[slot]]
+
+
+def slotted_tiles(pairs, tiles):
+    whole = pl.BlockSpec(memory_space=pltpu.VMEM)
     return pl.pallas_call(
-        pieces_kernel,
-        out_shape=jax.ShapeDtypeStruct((slot_total, channels, cells), jnp.bfloat16),
-        grid_spec=pltpu.PrefetchScalarGridSpec(
-            num_scalar_prefetch=1,
-            grid=(atm_blocks // per_step,),
-            in_specs=[
-                pl.BlockSpec((per_step, channels, cells), lambda s, _: (s, 0, 0)),
-                pl.BlockSpec((per_step, top_count, cells, cells), lambda s, _: (s, 0, 0, 0)),
-            ],
-            out_specs=pl.BlockSpec((slot_total, channels, cells), lambda s, _: (0, 0, 0)),
-        ),
+        slots_kernel,
+        out_shape=jax.ShapeDtypeStruct(pairs.shape + tiles.shape[1:], tiles.dtype),
+        in_specs=[pl.BlockSpec(memory_space=pltpu.SMEM), whole],
+        out_specs=whole,
         compiler_params=pltpu.CompilerParams(vmem_limit_bytes=VMEM_BYTES),
-    )(slot_index, state, tiles)
+    )(pairs, tiles)
 
 
 def adjoint_kernel(slot_ref, back_ref, tiles_ref, out_ref):
@@ -171,7 +157,9 @@
     scale_in,
     scale_out,
     id_ref,
-    received_ref,
+    state_at_ref,
+    states_ref,
+    slots_ref,
     mask_ref,
     goal_ref,
     w_in_ref,
@@ -186,20 +174,29 @@
     act_ref,
     out_ref,
 ):
-    slots = received_ref.shape[0]
+    slots = slots_ref.shape[0]
     ocean_blocks = goal_ref.shape[0]
     hidden, channels = w_in_t_ref.shape
-    cells = received_ref.shape[2]
+    cells = slots_ref.shape[2]
     group = math.gcd(ocean_blocks, 4)
     chunk = math.gcd(hidden, 256)
     total_ref[...] = jnp.zeros_like(total_ref)
     grads_ref[...] = jnp.zeros_like(grads_ref)
     out_ref[...] = jnp.zeros_like(out_ref)
 
-    @pl.loop(0, slots)
-    def _(slot):
-        block = id_ref[slot]
-        total_ref[block] += received_ref[slot].astype(jnp.float32)
+    batch = math.gcd(slots, 8)
+
+    @pl.loop(0, slots // batch)
+    def _(step):
+        places = [step * batch + b for b in range(batch)]
+        pieces = [
+            jnp.dot(
+                states_ref[state_at_ref[slot]], slots_ref[slot], preferred_element_type=jnp.float32
+            ).astype(jnp.bfloat16)
+            for slot in places
+        ]
+        for slot, piece in zip(places, pieces):
+            total_ref[id_ref[slot]] += piece.astype(jnp.float32)
 
     @pl.loop(0, ocean_blocks // group)
     def _(step):
@@ -251,8 +248,8 @@
             pieces_ref[p, :, hidden : hidden + 128] = jnp.zeros((8, 128), jnp.float32)
 
 
-def network(received, ids, wet_mask, target, w_in, w_out, scale_in, scale_out):
-    slots, channels, cells = received.shape
+def network(states, tiles, state_at, ids, wet_mask, target, w_in, w_out, scale_in, scale_out):
+    _, channels, cells = states.shape
     ocean_blocks, outputs, _ = target.shape
     hidden = w_in.shape[1]
     group = math.gcd(ocean_blocks, 4)
@@ -264,7 +261,7 @@
             jax.ShapeDtypeStruct((ocean_blocks, channels, cells), jnp.bfloat16),
             jax.ShapeDtypeStruct((channels // 8, 8, hidden + 128), jnp.float32),
         ),
-        in_specs=[pl.BlockSpec(memory_space=pltpu.SMEM)] + [whole] * 7,
+        in_specs=[pl.BlockSpec(memory_space=pltpu.SMEM)] * 2 + [whole] * 8,
         out_specs=(whole, whole),
         scratch_shapes=[
             pltpu.VMEM((ocean_blocks + 1, channels, cells), jnp.float32),
@@ -276,7 +273,9 @@
         compiler_params=pltpu.CompilerParams(vmem_limit_bytes=VMEM_BYTES),
     )(
         ids,
-        received,
+        state_at,
+        states,
+        tiles,
         wet_mask.astype(jnp.float32)[:, None, :],
         jnp.pad(target, ((0, 0), (0, 8 - outputs), (0, 0))),
         w_in,
@@ -483,6 +482,203 @@
     )(feat_grad, grads)
 
 
+def spread_kernel(
+    space_size,
+    columns,
+    member_size,
+    state_ref,
+    tiles_ref,
+    states_ref,
+    slots_ref,
+    tile_send,
+    tile_recv,
+    share_send,
+    share_recv,
+    line_send,
+    line_recv,
+    pair_send,
+    pair_recv,
+    own_sem,
+):
+    group, space, member = (lax.axis_index(name) for name in ("group", "space", "member"))
+    column = group * member_size + member
+    length = space_size // 2
+    place, core = space // 2, space % 2
+    size = state_ref.shape[0] // CHUNKS
+    share = tiles_ref.shape[1]
+
+    def along(j):
+        return lax.rem(space + j, space_size)
+
+    def across(i):
+        other = lax.rem(column + i, columns)
+        return other, {"group": other // member_size, "member": other % member_size}
+
+    barrier = pltpu.get_barrier_semaphore()
+    for j in range(1, space_size):
+        pl.semaphore_signal(barrier, inc=1, device_id={"space": along(j)}, device_id_type=MESH)
+    for i in range(1, columns):
+        pl.semaphore_signal(barrier, inc=1, device_id=across(i)[1], device_id_type=MESH)
+    pl.semaphore_wait(barrier, space_size + columns - 2)
+
+    def part(origin, owner):
+        return slots_ref.at[origin, pl.ds(owner * share, share)]
+
+    def tile(j, origin):
+        return pltpu.make_async_remote_copy(
+            src_ref=tiles_ref.at[along(j)],
+            dst_ref=part(origin, column),
+            send_sem=tile_send.at[j - 1],
+            recv_sem=tile_recv.at[j - 1],
+            device_id={"space": along(j)},
+            device_id_type=MESH,
+        )
+
+    def shared(i, j, owner):
+        origin = along(space_size - j)
+        return pltpu.make_async_remote_copy(
+            src_ref=tiles_ref.at[space] if j == 0 else part(origin, column),
+            dst_ref=part(origin, owner),
+            send_sem=share_send.at[i - 1, j],
+            recv_sem=share_recv.at[i - 1, j],
+            device_id=across(i)[1],
+            device_id_type=MESH,
+        )
+
+    def source(origin, own, c):
+        rows = pl.ds(c * size, size)
+        return state_ref.at[rows] if own else states_ref.at[origin, rows]
+
+    def line(way, hop, c, origin, own):
+        step = 1 if way == 0 else -1
+        return pltpu.make_async_remote_copy(
+            src_ref=source(origin, own, c),
+            dst_ref=states_ref.at[origin, pl.ds(c * size, size)],
+            send_sem=line_send.at[way, hop, c],
+            recv_sem=line_recv.at[way, hop, c],
+            device_id={"space": (place + step) * 2 + core},
+            device_id_type=MESH,
+        )
+
+    def pair(index, c, origin, own):
+        return pltpu.make_async_remote_copy(
+            src_ref=source(origin, own, c),
+            dst_ref=states_ref.at[origin, pl.ds(c * size, size)],
+            send_sem=pair_send.at[index, c],
+            recv_sem=pair_recv.at[index, c],
+            device_id={"space": place * 2 + 1 - core},
+            device_id_type=MESH,
+        )
+
+    def behind(way, hop):
+        at = place - 1 - hop if way == 0 else place + 1 + hop
+        return at, (at >= 0 if way == 0 else at < length)
+
+    ahead = (place < length - 1, place > 0)
+    for j in range(1, space_size):
+        tile(j, space).start()
+    own_state = pltpu.make_async_copy(state_ref, states_ref.at[space], own_sem.at[0])
+    own_tiles = pltpu.make_async_copy(tiles_ref.at[space], part(space, column), own_sem.at[1])
+    for i in range(1, columns):
+        shared(i, 0, column).start()
+    for c in range(CHUNKS):
+        for way in range(2):
+
+            @pl.when(ahead[way])
+            def _():
+                line(way, 0, c, space, True).start()
+
+        pair(0, c, space, True).start()
+    own_state.start()
+    own_tiles.start()
+
+    order = list(range(1, space_size))
+    hops = length - 1
+    for hop in range(hops):
+        for j in order[hop * len(order) // hops : (hop + 1) * len(order) // hops]:
+            tile(j, along(space_size - j)).wait_recv()
+            for i in range(1, columns):
+                shared(i, j, column).start()
+        for c in range(CHUNKS):
+            for way in range(2):
+                at, there = behind(way, hop)
+                origin = at * 2 + core
+
+                @pl.when(there)
+                def _():
+                    line(way, hop, c, origin, False).wait_recv()
+                    if hop + 1 < hops:
+
+                        @pl.when(ahead[way])
+                        def _():
+                            line(way, hop + 1, c, origin, False).start()
+
+                    pair(1 + way * hops + hop, c, origin, False).start()
+
+    own_state.wait()
+    own_tiles.wait()
+    for j in range(1, space_size):
+        tile(j, space).wait_send()
+    for i in range(1, columns):
+        for j in range(space_size):
+            shared(i, j, across(columns - i)[0]).wait_recv()
+            shared(i, j, column).wait_send()
+    for c in range(CHUNKS):
+        pair(0, c, space, True).wait_send()
+        pair(0, c, place * 2 + 1 - core, False).wait_recv()
+        for way in range(2):
+
+            @pl.when(ahead[way])
+            def _():
+                line(way, 0, c, space, True).wait_send()
+
+            for hop in range(hops):
+                at, there = behind(way, hop)
+                origin = at * 2 + core
+                index = 1 + way * hops + hop
+
+                @pl.when(there)
+                def _():
+                    if hop + 1 < hops:
+
+                        @pl.when(ahead[way])
+                        def _():
+                            line(way, hop + 1, c, origin, False).wait_send()
+
+                    pair(index, c, origin, False).wait_send()
+                    pair(index, c, at * 2 + 1 - core, False).wait_recv()
+
+
+def spread(state, tile_slots, space_size, columns, member_size):
+    hops = space_size // 2 - 1
+    _, share, cells, _ = tile_slots.shape
+    dma = pltpu.SemaphoreType.DMA
+    anywhere = pl.BlockSpec(memory_space=pl.ANY)
+    return pl.pallas_call(
+        lambda *refs: spread_kernel(space_size, columns, member_size, *refs),
+        out_shape=(
+            jax.ShapeDtypeStruct((space_size,) + state.shape, state.dtype),
+            jax.ShapeDtypeStruct((space_size, columns * share, cells, cells), tile_slots.dtype),
+        ),
+        in_specs=[anywhere, anywhere],
+        out_specs=(anywhere, anywhere),
+        scratch_shapes=[
+            dma((space_size - 1,)),
+            dma((space_size - 1,)),
+            dma((columns - 1, space_size)),
+            dma((columns - 1, space_size)),
+            dma((2, hops, CHUNKS)),
+            dma((2, hops, CHUNKS)),
+            dma((1 + 2 * hops, CHUNKS)),
+            dma((1 + 2 * hops, CHUNKS)),
+            dma((2,)),
+        ],
+        compiler_params=pltpu.CompilerParams(
+            collective_id=1, has_side_effects=True, vmem_limit_bytes=VMEM_BYTES
+        ),
+    )(state, tile_slots)
+
+
 def fused_body(atm_state, remap_tiles, dest_device, dest_block, wet_mask, target, w_in, w_out):
     space_size = lax.axis_size("space")
     member_size = lax.axis_size("member")
@@ -490,11 +686,12 @@
     ocean_blocks = wet_mask.shape[0]
     channels = atm_state.shape[2]
     pieces_fit = channels == 8 * space_size * member_size and w_in.shape[1] <= 16 * channels
-    if not pieces_fit or ocean_blocks % CHUNKS:
+    columns = lax.axis_size("group") * member_size
+    capacity = min(atm_blocks, max(2, 2 * atm_blocks * top_count // space_size))
+    if not pieces_fit or ocean_blocks % CHUNKS or atm_blocks % CHUNKS or capacity % columns:
         return general_body(
             atm_state, remap_tiles, dest_device, dest_block, wet_mask, target, w_in, w_out
         )
-    capacity = min(atm_blocks, max(2, 2 * atm_blocks * top_count // space_size))
     pair_count = atm_blocks * top_count
     slot_total = space_size * capacity
     dest_flat = dest_device.reshape(pair_count)
@@ -503,27 +700,38 @@
     )
     slot_rank = jnp.sum((jnp.cumsum(onehot, axis=0) - onehot) * onehot, axis=1)
     slot_index = dest_flat * capacity + slot_rank
-    send_ids = (
-        jnp.full((slot_total,), ocean_blocks, jnp.int32)
+    codes = (
+        jnp.full((slot_total,), ocean_blocks * pair_count, jnp.int32)
         .at[slot_index]
-        .set(dest_block.reshape(pair_count))
-    )
-    received_ids = lax.all_to_all(
-        send_ids.reshape(space_size, capacity), "space", split_axis=0, concat_axis=0, tiled=True
+        .set(dest_block.reshape(pair_count) * pair_count + jnp.arange(pair_count, dtype=jnp.int32))
+    ).reshape(space_size, capacity)
+    share = capacity // columns
+    column = lax.axis_index("group") * member_size + lax.axis_index("member")
+    mine = lax.dynamic_slice_in_dim(codes, column * share, share, axis=1)
+    tile_slots = slotted_tiles(
+        (mine % pair_count).reshape(-1), remap_tiles.reshape(pair_count, cells, cells)
+    ).reshape(space_size, share, cells, cells)
+    received_codes = lax.all_to_all(codes, "space", split_axis=0, concat_axis=0, tiled=True)
+    states, tiles = spread(atm_state[0], tile_slots, space_size, columns, member_size)
+    received_ids = (received_codes // pair_count).reshape(slot_total)
+    state_at = (
+        jnp.arange(space_size, dtype=jnp.int32)[:, None] * atm_blocks
+        + received_codes % pair_count // top_count
     ).reshape(slot_total)
-    outgoing = slotted_pieces(slot_index, atm_state[0], remap_tiles, slot_total)
-    received = lax.all_to_all(
-        outgoing.reshape(space_size, capacity, channels, cells),
-        "space",
-        split_axis=0,
-        concat_axis=0,
-        tiled=True,
-    ).reshape(slot_total, channels, cells)
     cell_total = member_size * space_size * ocean_blocks * cells
     scale_in = math.sqrt(w_in.shape[1] / cell_total)
     scale_out = 1.0 / math.sqrt(cell_total)
     feat_grad, grads = network(
-        received, received_ids, wet_mask, target[0], w_in, w_out, scale_in, scale_out
+        states.reshape(space_size * atm_blocks, channels, cells),
+        tiles.reshape(slot_total, cells, cells),
+        state_at,
+        received_ids,
+        wet_mask,
+        target[0],
+        w_in,
+        w_out,
+        scale_in,
+        scale_out,
     )
     gathered, summed = exchange(feat_grad, grads, space_size, member_size)
     owner = dest_flat * ocean_blocks + dest_block.reshape(pair_count)
@@ -537,7 +745,7 @@
 
 
 def solution(mesh):
-    body = fused_body if mesh.shape["level"] == 1 and mesh.shape["space"] % 2 == 0 else general_body
+    body = fused_body if mesh.shape["level"] == 1 and mesh.shape["space"] in (4, 6, 8) else general_body
     return jax.shard_map(
         body,
         mesh=mesh,

time: 243 us -> 221 us (0.909)
  waiting for transfers between devices: 92.2 us -> 0.01 us
  Pallas kernels: 128 us -> 199 us
  starting transfers between devices: 11.6 us -> 6.33 us
  local copies, waits for them, and re-layouts: 8.46 us -> 12.2 us
    all_to_all x2 -> x1, waiting for transfers between devices: 92.2 us -> 0.01 us  [fused_body(): lax.all_to_all(codes, 'space', split_axis=0, concat_axis=0, tiled=True)]
    pallas_call x1 -> x2, Pallas kernels: 3.73 us -> 66.5 us  [the longest x1 65.8 us: spread(): pl.pallas_call(lambda *refs: spread_kernel(space_size, columns, member_si...]
    all_to_all x2 -> x1, starting transfers between devices: 11.6 us -> 6.33 us  [fused_body(): lax.all_to_all(codes, 'space', split_axis=0, concat_axis=0, tiled=True)]
    pallas_call x1, Pallas kernels: 93.5 us -> 98.5 us  [exchange(): pl.pallas_call(lambda *refs: exchange_kernel(space_size, member_size, *re...]
    pallas_call x1, Pallas kernels: 24.1 us -> 27.8 us  [network(): pl.pallas_call(lambda *refs: network_kernel(scale_in, scale_out, *refs),...]
    unnamed x17 -> x13, local copies, waits for them, and re-layouts: 4.35 us -> 6.21 us
  transfers between devices with their start and end apart: 2 -> 1, of which waited for: 1 -> 0; matrix products, arithmetic and copies ran while one was open for 1% -> 2% of each run, Pallas kernels for 2% -> 30%
where the time goes in v3:
time: 221 us
  Pallas kernels  199 us (90%)
  local copies, waits for them, and re-layouts  12.2 us (6%)
  starting transfers between devices  6.33 us (3%)
  other arithmetic  2.68 us (1%)
    pallas_call x1, Pallas kernels, exchange(): pl.pallas_call(lambda *refs: exchange_kernel(space_size, member_size, *re...  98.5 us
    pallas_call x1, Pallas kernels, spread(): pl.pallas_call(lambda *refs: spread_kernel(space_size, columns, member_si...  65.8 us
    pallas_call x1, Pallas kernels, network(): pl.pallas_call(lambda *refs: network_kernel(scale_in, scale_out, *refs),...  27.8 us
    all_to_all x1, starting transfers between devices, fused_body(): lax.all_to_all(codes, 'space', split_axis=0, concat_axis=0, tiled=True)  6.33 us
    pallas_call x1, Pallas kernels, adjoint_of(): pl.pallas_call(adjoint_kernel, out_shape=jax.ShapeDtypeStruct((atm_blocks...  6.27 us
    unnamed x13, local copies, waits for them, and re-layouts  6.21 us
  transfers between devices with their start and end apart: 1, of which 0 were waited for; matrix products, arithmetic and copies ran while one was open for 2% of the time, Pallas kernels for 30%

profile of v3, /device:TPU:0, one launch (start us, length us, event | category | flops | bytes accessed | tf_op | source)
XLA Modules:
  0.0 221.0 jit_solution(7801139854041132141)
XLA Ops:
  0.6 0.0 copy-start.3
  0.6 0.0 copy-start.4
  0.7 0.8 broadcast_multiply_fusion
  1.4 0.8 copy.23
  2.2 0.1 copy.25
  2.2 0.1 mul.49
  2.3 0.8 copy.24
  3.1 0.1 reshape.83
  3.2 0.1 reshape.82
  3.3 0.1 fusion
  3.4 0.1 reduce_window_sum.11
  3.5 0.2 select_reduce_fusion
  3.7 0.8 scatter_custom_fusion
  4.4 0.7 all_to_all.8
  5.1 6.3 %all-to-all-start = ((s32[8,1,16]{2,1,0:T(1,128)}), s32[8,1,16]{2,1,0:T(1,128)S(1)}, u32[]{:S(2)}, u32[]{:S(2)}) async-start(s32[8,1,16]{2,1,0:T(1,128)} %bitcast.2), calls=%async_computation | async-start | bytes 8192 | tf_op jit(solution)/shard_map/all_to_all | solution.py:714
  11.4 0.1 reshape.84
  11.5 0.7 fusion.6
  12.2 0.1 pad.13.clone
  12.3 0.1 add_select_fusion
  12.4 0.1 maximum_maximum_fusion
  12.5 0.1 add.72
  12.5 0.1 add.73
  12.6 0.7 convert_element_type.11
  13.3 0.1 reshape.85.pair_ref
  13.4 0.2 copy.28.refs_9_
  13.6 1.1 copy.27
  14.7 0.9 pad.8.refs_5_
  15.6 0.0 copy-start
  15.6 1.6 copy-done
  17.2 0.6 shard_map.103
  17.8 0.0 copy-done.4
  17.9 65.8 %shard_map.104 = (bf16[8,16,128,128]{3,2,1,0:T(8,128)(2,1)S(1)}, bf16[8,16,128,128]{3,2,1,0:T(8,128)(2,1)}) custom-call(bf16[16,128,128]{2,1,0:T(8,128)(2,1)S(1)} %bitcast.30, bf16[8,4,128,128]{3,2,1,0:T(8,128)(2,1)S(1)} %bitcast.28), custom_call_target="tpu_custom_call" | custom-call | tf_op jit(solution)/shard_map/pallas_call | solution.py:657
  83.7 0.0 copy-start.2
  83.7 2.0 copy-done.2
  85.7 0.0 all-to-all-done
  85.7 0.5 broadcast.103
  86.2 0.7 reduce.3
  86.8 0.1 all_to_all.10
  86.9 0.0 copy-done.3
  87.0 0.0 copy-start.1
  87.0 27.8 %shard_map.105 = (bf16[32,128,128]{2,1,0:T(8,128)(2,1)S(1)}, f32[16,8,1152]{2,1,0:T(8,128)S(1)}) custom-call(s32[128]{0:T(128)S(1)} %get-tuple-element.18.refs_0_, s32[128]{0:T(128)S(1)} %get-tuple-element.17.refs_1_, bf16[128,128,128]{2,1,0:T(8,128)(2,1)} %bitcast.27, bf16[128,128,128]{2,1,0:T(8,128)(2,1)} %bitcast.33, f32[32,1,128]{2,1,0:T(1,128)S(1)} %bitcast.31, ...), custom_call_target="tpu_custom_call" | custom-call | tf_op jit(solution)/shard_map/pallas_call | solution.py:258
  114.8 98.5 %shard_map.106 = (bf16[8,32,128,128]{3,2,1,0:T(8,128)(2,1)}, f32[16,8,1152]{2,1,0:T(8,128)S(1)}) custom-call(bf16[32,128,128]{2,1,0:T(8,128)(2,1)S(1)} %get-tuple-element.11.refs_0_, f32[16,8,1152]{2,1,0:T(8,128)S(1)} %get-tuple-element.12.refs_1_), custom_call_target="tpu_custom_call" | custom-call | tf_op jit(solution)/shard_map/pallas_call | solution.py:458
  213.3 0.6 slice_bitcast_fusion.1
  213.9 0.8 slice_bitcast_fusion
  214.7 0.0 copy-done.1
  214.7 6.3 %shard_map.107 = f32[16,128,128]{2,1,0:T(8,128)} custom-call(s32[64]{0:T(128)S(1)} %get-tuple-element.20.slot_ref, bf16[256,128,128]{2,1,0:T(8,128)(2,1)} %bitcast.32, bf16[16,4,128,128]{3,2,1,0:T(8,128)(2,1)S(1)} %copy-done.1), custom_call_target="tpu_custom_call" | custom-call | tf_op jit(solution)/shard_map/pallas_call | solution.py:140
  (5 shorter events, 0.0 us)
Async XLA Ops:
  0.6 86.3 %copy-start.3 = (bf16[128,1024]{1,0:T(8,128)(2,1)S(1)}, bf16[128,1024]{1,0:T(8,128)(2,1)}, u32[]{:S(2)}) copy-start(bf16[128,1024]{1,0:T(8,128)(2,1)} %refs_6_.1) | copy-start | bytes 786436
  0.6 17.2 %copy-start.4 = (bf16[1,16,128,128]{3,2,1,0:T(8,128)(2,1)S(1)}, bf16[1,16,128,128]{3,2,1,0:T(8,128)(2,1)}, u32[]{:S(2)}) copy-start(bf16[1,16,128,128]{3,2,1,0:T(8,128)(2,1)} %param.8) | copy-start | bytes 1572868
  5.1 80.5 %all-to-all-start = ((s32[8,1,16]{2,1,0:T(1,128)}), s32[8,1,16]{2,1,0:T(1,128)S(1)}, u32[]{:S(2)}, u32[]{:S(2)}) async-start(s32[8,1,16]{2,1,0:T(1,128)} %bitcast.2), calls=%async_computation | async-start | bytes 8192 | tf_op jit(solution)/shard_map/all_to_all | solution.py:714
  15.6 1.6 copy-start
  83.7 2.0 copy-start.2
  87.0 127.8 %copy-start.1 = (bf16[16,4,128,128]{3,2,1,0:T(8,128)(2,1)S(1)}, bf16[16,4,128,128]{3,2,1,0:T(8,128)(2,1)}, u32[]{:S(2)}) copy-start(bf16[16,4,128,128]{3,2,1,0:T(8,128)(2,1)} %tiles_ref.1) | copy-start | bytes 6291460

commit v4 on v3

--- a/solution.py
+++ b/solution.py
@@ -296,12 +296,14 @@
     grads_ref,
     all_ref,
     sums_ref,
-    inbox,
+    team_box,
+    partial,
+    place_box,
     total,
-    term_send,
-    term_recv,
-    sum_send,
-    sum_recv,
+    team_send,
+    team_recv,
+    place_send,
+    place_recv,
     line_send,
     line_recv,
     pair_send,
@@ -309,41 +311,82 @@
     own_sem,
 ):
     space, member = lax.axis_index("space"), lax.axis_index("member")
-    ranks = space_size * member_size
-    rank = member * space_size + space
     length = space_size // 2
     place, core = space // 2, space % 2
     size = feat_ref.shape[0] // CHUNKS
 
-    def peer(i):
-        other = lax.rem(rank + i, ranks)
-        return other, {"space": other % space_size, "member": other // space_size}
+    teams = 2 * member_size
+    team = member * 2 + core
+
+    def mate(i):
+        other = lax.rem(team + i, teams)
+        return other, {"space": place * 2 + other % 2, "member": other // 2}
+
+    def far(i):
+        other = lax.rem(place + i, length)
+        return other, {"space": other * 2 + core}
 
     barrier = pltpu.get_barrier_semaphore()
-    for i in range(1, ranks):
-        pl.semaphore_signal(barrier, inc=1, device_id=peer(i)[1], device_id_type=MESH)
-    pl.semaphore_wait(barrier, ranks - 1)
-
-    def term(i):
-        other, device = peer(i)
+    for i in range(1, teams):
+        pl.semaphore_signal(barrier, inc=1, device_id=mate(i)[1], device_id_type=MESH)
+    for i in range(1, length):
+        pl.semaphore_signal(barrier, inc=1, device_id=far(i)[1], device_id_type=MESH)
+    pl.semaphore_wait(barrier, teams + length - 2)
+
+    def team_copy(back, i, owner):
+        other, device = mate(i)
+        rows = pl.ds((owner if back else other) * length, length)
         return pltpu.make_async_remote_copy(
-            src_ref=grads_ref.at[other],
-            dst_ref=inbox.at[i - 1],
-            send_sem=term_send.at[i - 1],
-            recv_sem=term_recv.at[i - 1],
+            src_ref=sums_ref.at[rows] if back else grads_ref.at[rows],
+            dst_ref=sums_ref.at[rows] if back else team_box.at[i - 1],
+            send_sem=team_send.at[back, i - 1],
+            recv_sem=team_recv.at[back, i - 1],
             device_id=device,
             device_id_type=MESH,
         )
 
-    def piece(i, owner):
+    def place_copy(back, i, owner):
+        other, device = far(i)
         return pltpu.make_async_remote_copy(
-            src_ref=total,
-            dst_ref=sums_ref.at[owner],
-            send_sem=sum_send.at[i - 1],
-            recv_sem=sum_recv.at[i - 1],
-            device_id=peer(i)[1],
+            src_ref=total if back else partial.at[other],
+            dst_ref=sums_ref.at[team * length + owner] if back else place_box.at[i - 1],
+            send_sem=place_send.at[back, i - 1],
+            recv_sem=place_recv.at[back, i - 1],
+            device_id=device,
             device_id_type=MESH,
         )
+
+    own_sum = pltpu.make_async_copy(total, sums_ref.at[team * length + place], own_sem.at[1])
+
+    def sum_team():
+        for i in range(1, teams):
+            team_copy(0, i, team).wait_recv()
+        value = grads_ref[pl.ds(team * length, length)]
+        for i in range(1, teams):
+            value += team_box[i - 1]
+        partial[...] = value
+        for i in range(1, length):
+            place_copy(0, i, place).start()
+
+    def sum_places():
+        for i in range(1, length):
+            place_copy(0, i, place).wait_recv()
+        value = partial[place]
+        for i in range(1, length):
+            value += place_box[i - 1]
+        total[...] = value
+        for i in range(1, length):
+            place_copy(1, i, place).start()
+        own_sum.start()
+
+    def share_sums():
+        for i in range(1, length):
+            place_copy(1, i, far(length - i)[0]).wait_recv()
+        own_sum.wait()
+        for i in range(1, teams):
+            team_copy(1, i, team).start()
+
+    phases = [sum_team, sum_places, share_sums]
 
     def source(origin, own, c):
         rows = pl.ds(c * size, size)
@@ -376,6 +419,8 @@
 
     ahead = (place < length - 1, place > 0)
     own_copy = pltpu.make_async_copy(feat_ref, all_ref.at[space], own_sem.at[0])
+    for i in range(1, teams):
+        team_copy(0, i, team).start()
     for c in range(CHUNKS):
         for way in range(2):
 
@@ -383,8 +428,6 @@
             def _():
                 line(way, 0, c, space, True).start()
 
-    for i in range(1, ranks):
-        term(i).start()
     for c in range(CHUNKS):
         pair(0, c, space, True).start()
     own_copy.start()
@@ -406,24 +449,17 @@
 
                     pair(1 + way * (length - 1) + hop, c, origin, False).start()
 
-        if hop == 0:
-            for i in range(1, ranks):
-                term(i).wait_recv()
-            value = grads_ref[rank]
-            for i in range(1, ranks):
-                value += inbox[i - 1]
-            total[...] = value
-            for i in range(1, ranks):
-                piece(i, rank).start()
-            own_sum = pltpu.make_async_copy(total, sums_ref.at[rank], own_sem.at[1])
-            own_sum.start()
+            if phases:
+                phases.pop(0)()
 
     own_copy.wait()
-    own_sum.wait()
-    for i in range(1, ranks):
-        piece(i, lax.rem(rank + ranks - i, ranks)).wait_recv()
-        piece(i, rank).wait_send()
-        term(i).wait_send()
+    for back in range(2):
+        for i in range(1, teams):
+            team_copy(back, i, team).wait_send()
+        for i in range(1, length):
+            place_copy(back, i, place).wait_send()
+    for i in range(1, teams):
+        team_copy(1, i, mate(teams - i)[0]).wait_recv()
     for c in range(CHUNKS):
         pair(0, c, space, True).wait_send()
         pair(0, c, place * 2 + 1 - core, False).wait_recv()
@@ -451,8 +487,9 @@
 
 
 def exchange(feat_grad, grads, space_size, member_size):
-    peers = space_size * member_size - 1
-    hops = max(1, space_size // 2 - 1)
+    teams, length = 2 * member_size, space_size // 2
+    hops = length - 1
+    piece = grads.shape[1:]
     dma = pltpu.SemaphoreType.DMA
     anywhere = pl.BlockSpec(memory_space=pl.ANY)
     return pl.pallas_call(
@@ -464,12 +501,14 @@
         in_specs=[anywhere, pl.BlockSpec(memory_space=pltpu.VMEM)],
         out_specs=(anywhere, anywhere),
         scratch_shapes=[
-            pltpu.VMEM((peers,) + grads.shape[1:], grads.dtype),
-            pltpu.VMEM(grads.shape[1:], grads.dtype),
-            dma((peers,)),
-            dma((peers,)),
-            dma((peers,)),
-            dma((peers,)),
+            pltpu.VMEM((teams - 1, length) + piece, grads.dtype),
+            pltpu.VMEM((length,) + piece, grads.dtype),
+            pltpu.VMEM((length - 1,) + piece, grads.dtype),
+            pltpu.VMEM(piece, grads.dtype),
+            dma((2, teams - 1)),
+            dma((2, teams - 1)),
+            dma((2, length - 1)),
+            dma((2, length - 1)),
             dma((2, hops, CHUNKS)),
             dma((2, hops, CHUNKS)),
             dma((1 + 2 * hops, CHUNKS)),
@@ -488,8 +527,12 @@
     member_size,
     state_ref,
     tiles_ref,
+    codes_ref,
     states_ref,
     slots_ref,
+    all_codes_ref,
+    code_send,
+    code_recv,
     tile_send,
     tile_recv,
     share_send,
@@ -534,6 +577,16 @@
             device_id_type=MESH,
         )
 
+    def code(j, origin):
+        return pltpu.make_async_remote_copy(
+            src_ref=codes_ref.at[along(j)],
+            dst_ref=all_codes_ref.at[origin],
+            send_sem=code_send.at[j - 1],
+            recv_sem=code_recv.at[j - 1],
+            device_id={"space": along(j)},
+            device_id_type=MESH,
+        )
+
     def shared(i, j, owner):
         origin = along(space_size - j)
         return pltpu.make_async_remote_copy(
@@ -576,7 +629,10 @@
 
     ahead = (place < length - 1, place > 0)
     for j in range(1, space_size):
+        code(j, space).start()
         tile(j, space).start()
+    own_codes = pltpu.make_async_copy(codes_ref.at[space], all_codes_ref.at[space], own_sem.at[2])
+    own_codes.start()
     own_state = pltpu.make_async_copy(state_ref, states_ref.at[space], own_sem.at[0])
     own_tiles = pltpu.make_async_copy(tiles_ref.at[space], part(space, column), own_sem.at[1])
     for i in range(1, columns):
@@ -617,7 +673,10 @@
 
     own_state.wait()
     own_tiles.wait()
+    own_codes.wait()
     for j in range(1, space_size):
+        code(j, along(space_size - j)).wait_recv()
+        code(j, space).wait_send()
         tile(j, space).wait_send()
     for i in range(1, columns):
         for j in range(space_size):
@@ -649,7 +708,7 @@
                     pair(index, c, at * 2 + 1 - core, False).wait_recv()
 
 
-def spread(state, tile_slots, space_size, columns, member_size):
+def spread(state, tile_slots, codes, space_size, columns, member_size):
     hops = space_size // 2 - 1
     _, share, cells, _ = tile_slots.shape
     dma = pltpu.SemaphoreType.DMA
@@ -659,10 +718,13 @@
         out_shape=(
             jax.ShapeDtypeStruct((space_size,) + state.shape, state.dtype),
             jax.ShapeDtypeStruct((space_size, columns * share, cells, cells), tile_slots.dtype),
+            jax.ShapeDtypeStruct(codes.shape, codes.dtype),
         ),
-        in_specs=[anywhere, anywhere],
-        out_specs=(anywhere, anywhere),
+        in_specs=[anywhere] * 3,
+        out_specs=(anywhere,) * 3,
         scratch_shapes=[
+            dma((space_size - 1,)),
+            dma((space_size - 1,)),
             dma((space_size - 1,)),
             dma((space_size - 1,)),
             dma((columns - 1, space_size)),
@@ -671,12 +733,12 @@
             dma((2, hops, CHUNKS)),
             dma((1 + 2 * hops, CHUNKS)),
             dma((1 + 2 * hops, CHUNKS)),
-            dma((2,)),
+            dma((3,)),
         ],
         compiler_params=pltpu.CompilerParams(
             collective_id=1, has_side_effects=True, vmem_limit_bytes=VMEM_BYTES
         ),
-    )(state, tile_slots)
+    )(state, tile_slots, codes)
 
 
 def fused_body(atm_state, remap_tiles, dest_device, dest_block, wet_mask, target, w_in, w_out):
@@ -711,8 +773,13 @@
     tile_slots = slotted_tiles(
         (mine % pair_count).reshape(-1), remap_tiles.reshape(pair_count, cells, cells)
     ).reshape(space_size, share, cells, cells)
-    received_codes = lax.all_to_all(codes, "space", split_axis=0, concat_axis=0, tiled=True)
-    states, tiles = spread(atm_state[0], tile_slots, space_size, columns, member_size)
+    wide_codes = jnp.broadcast_to(
+        jnp.pad(codes, ((0, 0), (0, -capacity % 128)))[:, None, :], (space_size, 8, -(-capacity // 128) * 128)
+    )
+    states, tiles, received_codes = spread(
+        atm_state[0], tile_slots, wide_codes, space_size, columns, member_size
+    )
+    received_codes = received_codes[:, 0, :capacity]
     received_ids = (received_codes // pair_count).reshape(slot_total)
     state_at = (
         jnp.arange(space_size, dtype=jnp.int32)[:, None] * atm_blocks
@@ -745,7 +812,7 @@
 
 
 def solution(mesh):
-    body = fused_body if mesh.shape["level"] == 1 and mesh.shape["space"] in (4, 6, 8) else general_body
+    body = fused_body if mesh.shape["level"] == 1 and mesh.shape["space"] in (6, 8) else general_body
     return jax.shard_map(
         body,
         mesh=mesh,

time: 221 us -> 200 us (0.905)
  Pallas kernels: 199 us -> 186 us
  starting transfers between devices: 6.33 us -> 0 us
    pallas_call x1, Pallas kernels: 98.5 us -> 83.5 us  [exchange(): pl.pallas_call(lambda *refs: exchange_kernel(space_size, member_size, *re...]
    all_to_all x1 -> x0, starting transfers between devices: 6.33 us -> none  [fused_body(): lax.all_to_all(codes, 'space', split_axis=0, concat_axis=0, tiled=True)]
  transfers between devices with their start and end apart: 1 -> 0, of which waited for: 0 -> 0; matrix products, arithmetic and copies ran while one was open for 2% -> 0% of each run, Pallas kernels for 30% -> 0%
where the time goes in v4:
time: 200 us
  Pallas kernels  186 us (93%)
  local copies, waits for them, and re-layouts  11 us (6%)
  other arithmetic  2.04 us (1%)
    pallas_call x1, Pallas kernels, exchange(): pl.pallas_call(lambda *refs: exchange_kernel(space_size, member_size, *re...  83.5 us
    pallas_call x1, Pallas kernels, spread(): pl.pallas_call(lambda *refs: spread_kernel(space_size, columns, member_si...  67.8 us
    pallas_call x1, Pallas kernels, network(): pl.pallas_call(lambda *refs: network_kernel(scale_in, scale_out, *refs),...  27.8 us
    pallas_call x1, Pallas kernels, adjoint_of(): pl.pallas_call(adjoint_kernel, out_shape=jax.ShapeDtypeStruct((atm_blocks...  6.26 us
    unnamed x13, local copies, waits for them, and re-layouts  6.21 us

profile of v4, /device:TPU:0, one launch (start us, length us, event | category | flops | bytes accessed | tf_op | source)
XLA Modules:
  0.0 199.8 jit_solution(15572789432297433840)
XLA Ops:
  0.6 0.0 copy-start.3
  0.6 0.0 copy-start.4
  0.7 0.1 pad.18.clone
  0.7 0.8 broadcast_multiply_fusion
  1.5 0.1 add.77
  1.6 0.1 add.78
  1.7 0.1 copy.25
  1.8 0.1 mul.49
  1.9 0.8 copy.24
  2.6 0.1 reshape.81
  2.7 0.8 copy.23
  3.5 0.1 reshape.80
  3.6 0.7 convert_element_type.11
  4.3 0.1 fusion
  4.4 0.1 reduce_window_sum.11
  4.5 0.2 select_reduce_fusion
  4.7 0.8 scatter_custom_fusion
  5.4 0.1 reshape.82
  5.5 0.1 add_select_fusion
  5.6 0.1 reshape.83.pair_ref
  5.7 0.7 fusion.6
  6.4 0.1 maximum_maximum_fusion
  6.5 0.9 pad.13.refs_5_
  7.3 0.2 copy.27.refs_9_
  7.5 1.1 copy.26
  8.6 0.0 copy-start
  8.7 1.6 copy-done
  10.2 0.6 shard_map.103
  10.9 0.0 copy-done.4
  10.9 67.8 %shard_map.104 = (bf16[8,16,128,128]{3,2,1,0:T(8,128)(2,1)S(1)}, bf16[8,16,128,128]{3,2,1,0:T(8,128)(2,1)}, s32[8,8,128]{2,1,0:T(8,128)S(1)}) custom-call(bf16[16,128,128]{2,1,0:T(8,128)(2,1)S(1)} %bitcast.29, bf16[8,4,128,128]{3,2,1,0:T(8,128)(2,1)S(1)} %bitcast.27, s32[8,8,128]{2,1,0:T(8,128)S(1)} %broadcast_in_dim.22.refs_2_), custom_call_target="tpu_custom_call" | custom-call | tf_op jit(solution)/shard_map/pallas_call | solution.py:716
  78.7 0.0 copy-start.2
  78.7 2.0 copy-done.2
  80.7 0.1 squeeze.10
  80.8 0.0 copy-done.3
  80.8 0.0 copy-start.1
  80.8 27.8 %shard_map.105 = (bf16[32,128,128]{2,1,0:T(8,128)(2,1)S(1)}, f32[16,8,1152]{2,1,0:T(8,128)S(1)}) custom-call(s32[128]{0:T(128)S(1)} %get-tuple-element.20.refs_0_, s32[128]{0:T(128)S(1)} %get-tuple-element.19.refs_1_, bf16[128,128,128]{2,1,0:T(8,128)(2,1)} %bitcast.26, bf16[128,128,128]{2,1,0:T(8,128)(2,1)} %bitcast.32, f32[32,1,128]{2,1,0:T(1,128)S(1)} %bitcast.30, ...), custom_call_target="tpu_custom_call" | custom-call | tf_op jit(solution)/shard_map/pallas_call | solution.py:258
  108.6 83.5 %shard_map.106 = (bf16[8,32,128,128]{3,2,1,0:T(8,128)(2,1)}, f32[16,8,1152]{2,1,0:T(8,128)S(1)}) custom-call(bf16[32,128,128]{2,1,0:T(8,128)(2,1)S(1)} %get-tuple-element.13.refs_0_, f32[16,8,1152]{2,1,0:T(8,128)S(1)} %get-tuple-element.14.refs_1_), custom_call_target="tpu_custom_call" | custom-call | tf_op jit(solution)/shard_map/pallas_call | solution.py:495
  192.1 0.0 copy-done.1
  192.1 6.3 %shard_map.107 = f32[16,128,128]{2,1,0:T(8,128)} custom-call(s32[64]{0:T(128)S(1)} %get-tuple-element.22.slot_ref, bf16[256,128,128]{2,1,0:T(8,128)(2,1)} %bitcast.31, bf16[16,4,128,128]{3,2,1,0:T(8,128)(2,1)S(1)} %copy-done.1), custom_call_target="tpu_custom_call" | custom-call | tf_op jit(solution)/shard_map/pallas_call | solution.py:140
  198.4 0.6 slice_bitcast_fusion.1
  199.0 0.8 slice_bitcast_fusion
  (8 shorter events, 0.1 us)
Async XLA Ops:
  0.6 80.1 %copy-start.3 = (bf16[128,1024]{1,0:T(8,128)(2,1)S(1)}, bf16[128,1024]{1,0:T(8,128)(2,1)}, u32[]{:S(2)}) copy-start(bf16[128,1024]{1,0:T(8,128)(2,1)} %refs_6_.1) | copy-start | bytes 786436
  0.6 10.3 %copy-start.4 = (bf16[1,16,128,128]{3,2,1,0:T(8,128)(2,1)S(1)}, bf16[1,16,128,128]{3,2,1,0:T(8,128)(2,1)}, u32[]{:S(2)}) copy-start(bf16[1,16,128,128]{3,2,1,0:T(8,128)(2,1)} %param.8) | copy-start | bytes 1572868
  8.6 1.6 copy-start
  78.7 2.0 copy-start.2
  80.8 111.3 %copy-start.1 = (bf16[16,4,128,128]{3,2,1,0:T(8,128)(2,1)S(1)}, bf16[16,4,128,128]{3,2,1,0:T(8,128)(2,1)}, u32[]{:S(2)}) copy-start(bf16[16,4,128,128]{3,2,1,0:T(8,128)(2,1)} %tiles_ref.1) | copy-start | bytes 6291460

commit v5 on v4

--- a/solution.py
+++ b/solution.py
@@ -153,37 +153,9 @@
     )(slot_index, returned, tiles)
 
 
-def network_kernel(
-    scale_in,
-    scale_out,
-    id_ref,
-    state_at_ref,
-    states_ref,
-    slots_ref,
-    mask_ref,
-    goal_ref,
-    w_in_ref,
-    w_in_t_ref,
-    w_out_t_ref,
-    w_out_3_ref,
-    grad_ref,
-    pieces_ref,
-    total_ref,
-    grads_ref,
-    pre_ref,
-    act_ref,
-    out_ref,
-):
+def features_kernel(id_ref, state_at_ref, states_ref, slots_ref, feat_ref, total_ref):
     slots = slots_ref.shape[0]
-    ocean_blocks = goal_ref.shape[0]
-    hidden, channels = w_in_t_ref.shape
-    cells = slots_ref.shape[2]
-    group = math.gcd(ocean_blocks, 4)
-    chunk = math.gcd(hidden, 256)
     total_ref[...] = jnp.zeros_like(total_ref)
-    grads_ref[...] = jnp.zeros_like(grads_ref)
-    out_ref[...] = jnp.zeros_like(out_ref)
-
     batch = math.gcd(slots, 8)
 
     @pl.loop(0, slots // batch)
@@ -198,93 +170,23 @@
         for slot, piece in zip(places, pieces):
             total_ref[id_ref[slot]] += piece.astype(jnp.float32)
 
-    @pl.loop(0, ocean_blocks // group)
-    def _(step):
-        first = step * group
-        feat = jnp.concatenate(
-            [total_ref[first + g].astype(jnp.bfloat16) for g in range(group)], axis=1
-        )
-        predicted = jnp.zeros((8, group * cells), jnp.float32)
-        for h in range(0, hidden, chunk):
-            rows = slice(h, h + chunk)
-            pre = jnp.dot(w_in_t_ref[rows], feat, preferred_element_type=jnp.float32)
-            pre_ref[rows] = pre
-            act = (pre * jax.nn.sigmoid(pre)).astype(jnp.bfloat16)
-            act_ref[rows] = act
-            predicted += jnp.dot(w_out_t_ref[:, rows], act, preferred_element_type=jnp.float32)
-        goal = jnp.concatenate([goal_ref[first + g] for g in range(group)], axis=1)
-        mask = jnp.concatenate([mask_ref[first + g] for g in range(group)], axis=1)
-        misfit = mask * (predicted - goal)
-        high = misfit.astype(jnp.bfloat16).astype(jnp.float32)
-        rest = misfit - high
-        middle = rest.astype(jnp.bfloat16).astype(jnp.float32)
-        low = rest - middle
-        misfit_3 = jnp.concatenate([high, middle, low, jnp.zeros_like(low)], axis=0).astype(
-            jnp.bfloat16
-        )
-        feat_grad = jnp.zeros((channels, group * cells), jnp.float32)
-        for h in range(0, hidden, chunk):
-            rows = slice(h, h + chunk)
-            act_grad = jnp.dot(w_out_3_ref[rows], misfit_3, preferred_element_type=jnp.float32)
-            pre = pre_ref[rows]
-            gate = jax.nn.sigmoid(pre)
-            pre_grad = (act_grad * gate * (1.0 + pre * (1.0 - gate))).astype(jnp.bfloat16)
-            feat_grad += jnp.dot(w_in_ref[:, rows], pre_grad, preferred_element_type=jnp.float32)
-            grads_ref[:, rows] += lax.dot_general(
-                feat, pre_grad, (((1,), (1,)), ((), ())), preferred_element_type=jnp.float32
-            )
-            out_ref[:, rows] += lax.dot_general(
-                misfit_3, act_ref[rows], (((1,), (1,)), ((), ())), preferred_element_type=jnp.float32
-            )
-        for g in range(group):
-            grad_ref[first + g] = feat_grad[:, g * cells : (g + 1) * cells].astype(jnp.bfloat16)
-
-    out = scale_out * (out_ref[0:8] + out_ref[8:16] + out_ref[16:24])
-    for p in range(pieces_ref.shape[0]):
-        pieces_ref[p, :, 0:hidden] = scale_in * grads_ref[8 * p : 8 * p + 8]
-        if (p + 1) * 128 <= hidden:
-            pieces_ref[p, :, hidden : hidden + 128] = out[:, p * 128 : (p + 1) * 128]
-        else:
-            pieces_ref[p, :, hidden : hidden + 128] = jnp.zeros((8, 128), jnp.float32)
-
-
-def network(states, tiles, state_at, ids, wet_mask, target, w_in, w_out, scale_in, scale_out):
+    feat_ref[...] = total_ref[0 : feat_ref.shape[0]].astype(jnp.bfloat16)
+
+
+def features_of(states, tiles, state_at, ids, ocean_blocks):
     _, channels, cells = states.shape
-    ocean_blocks, outputs, _ = target.shape
-    hidden = w_in.shape[1]
-    group = math.gcd(ocean_blocks, 4)
-    padded = jnp.pad(w_out, ((0, 0), (0, 8 - outputs)))
     whole = pl.BlockSpec(memory_space=pltpu.VMEM)
     return pl.pallas_call(
-        lambda *refs: network_kernel(scale_in, scale_out, *refs),
-        out_shape=(
-            jax.ShapeDtypeStruct((ocean_blocks, channels, cells), jnp.bfloat16),
-            jax.ShapeDtypeStruct((channels // 8, 8, hidden + 128), jnp.float32),
-        ),
-        in_specs=[pl.BlockSpec(memory_space=pltpu.SMEM)] * 2 + [whole] * 8,
-        out_specs=(whole, whole),
-        scratch_shapes=[
-            pltpu.VMEM((ocean_blocks + 1, channels, cells), jnp.float32),
-            pltpu.VMEM((channels, hidden), jnp.float32),
-            pltpu.VMEM((hidden, group * cells), jnp.float32),
-            pltpu.VMEM((hidden, group * cells), jnp.bfloat16),
-            pltpu.VMEM((32, hidden), jnp.float32),
-        ],
+        features_kernel,
+        out_shape=jax.ShapeDtypeStruct((ocean_blocks, channels, cells), jnp.bfloat16),
+        in_specs=[pl.BlockSpec(memory_space=pltpu.SMEM)] * 2 + [whole] * 2,
+        out_specs=whole,
+        scratch_shapes=[pltpu.VMEM((ocean_blocks + 1, channels, cells), jnp.float32)],
         compiler_params=pltpu.CompilerParams(vmem_limit_bytes=VMEM_BYTES),
-    )(
-        ids,
-        state_at,
-        states,
-        tiles,
-        wet_mask.astype(jnp.float32)[:, None, :],
-        jnp.pad(target, ((0, 0), (0, 8 - outputs), (0, 0))),
-        w_in,
-        w_in.T,
-        padded.T,
-        jnp.concatenate([padded, padded, padded, jnp.zeros_like(padded)], axis=1),
-    )
-
-
+    )(ids, state_at, states, tiles)
+
+
+PARTS = 4
 CHUNKS = 2
 MESH = pl.DeviceIdType.MESH
 
@@ -292,10 +194,23 @@
 def exchange_kernel(
     space_size,
     member_size,
+    scale_in,
+    scale_out,
+    features_ref,
+    mask_ref,
+    goal_ref,
+    w_in_ref,
+    w_in_t_ref,
+    w_out_t_ref,
+    w_out_3_ref,
+    all_ref,
+    sums_ref,
     feat_ref,
     grads_ref,
-    all_ref,
-    sums_ref,
+    in_ref,
+    pre_ref,
+    act_ref,
+    out_ref,
     team_box,
     partial,
     place_box,
@@ -313,7 +228,7 @@
     space, member = lax.axis_index("space"), lax.axis_index("member")
     length = space_size // 2
     place, core = space // 2, space % 2
-    size = feat_ref.shape[0] // CHUNKS
+    size = feat_ref.shape[0] // PARTS
 
     teams = 2 * member_size
     team = member * 2 + core
@@ -419,21 +334,78 @@
 
     ahead = (place < length - 1, place > 0)
     own_copy = pltpu.make_async_copy(feat_ref, all_ref.at[space], own_sem.at[0])
-    for i in range(1, teams):
-        team_copy(0, i, team).start()
-    for c in range(CHUNKS):
+    hidden, channels = w_in_t_ref.shape
+    cells = feat_ref.shape[2]
+    group = math.gcd(size, 4)
+    chunk = math.gcd(hidden, 256)
+    in_ref[...] = jnp.zeros_like(in_ref)
+    out_ref[...] = jnp.zeros_like(out_ref)
+
+    @pl.loop(0, PARTS)
+    def _(c):
+        @pl.loop(c * (size // group), (c + 1) * (size // group))
+        def _(step):
+            first = step * group
+            feat = jnp.concatenate(
+                [features_ref[first + g] for g in range(group)], axis=1
+            )
+            predicted = jnp.zeros((8, group * cells), jnp.float32)
+            for h in range(0, hidden, chunk):
+                rows = slice(h, h + chunk)
+                pre = jnp.dot(w_in_t_ref[rows], feat, preferred_element_type=jnp.float32)
+                pre_ref[rows] = pre
+                act = (pre * jax.nn.sigmoid(pre)).astype(jnp.bfloat16)
+                act_ref[rows] = act
+                predicted += jnp.dot(w_out_t_ref[:, rows], act, preferred_element_type=jnp.float32)
+            goal = jnp.concatenate([goal_ref[first + g] for g in range(group)], axis=1)
+            mask = jnp.concatenate([mask_ref[first + g] for g in range(group)], axis=1)
+            misfit = mask * (predicted - goal)
+            high = misfit.astype(jnp.bfloat16).astype(jnp.float32)
+            rest = misfit - high
+            middle = rest.astype(jnp.bfloat16).astype(jnp.float32)
+            low = rest - middle
+            misfit_3 = jnp.concatenate([high, middle, low, jnp.zeros_like(low)], axis=0).astype(
+                jnp.bfloat16
+            )
+            feat_grad = jnp.zeros((channels, group * cells), jnp.float32)
+            for h in range(0, hidden, chunk):
+                rows = slice(h, h + chunk)
+                act_grad = jnp.dot(w_out_3_ref[rows], misfit_3, preferred_element_type=jnp.float32)
+                pre = pre_ref[rows]
+                gate = jax.nn.sigmoid(pre)
+                pre_grad = (act_grad * gate * (1.0 + pre * (1.0 - gate))).astype(jnp.bfloat16)
+                feat_grad += jnp.dot(w_in_ref[:, rows], pre_grad, preferred_element_type=jnp.float32)
+                in_ref[:, rows] += lax.dot_general(
+                    feat, pre_grad, (((1,), (1,)), ((), ())), preferred_element_type=jnp.float32
+                )
+                out_ref[:, rows] += lax.dot_general(
+                    misfit_3, act_ref[rows], (((1,), (1,)), ((), ())), preferred_element_type=jnp.float32
+                )
+            for g in range(group):
+                feat_ref[first + g] = feat_grad[:, g * cells : (g + 1) * cells].astype(jnp.bfloat16)
+
         for way in range(2):
 
             @pl.when(ahead[way])
             def _():
                 line(way, 0, c, space, True).start()
 
-    for c in range(CHUNKS):
         pair(0, c, space, True).start()
+
+    out = scale_out * (out_ref[0:8] + out_ref[8:16] + out_ref[16:24])
+    for p in range(grads_ref.shape[0]):
+        grads_ref[p, :, 0:hidden] = scale_in * in_ref[8 * p : 8 * p + 8]
+        if (p + 1) * 128 <= hidden:
+            grads_ref[p, :, hidden : hidden + 128] = out[:, p * 128 : (p + 1) * 128]
+        else:
+            grads_ref[p, :, hidden : hidden + 128] = jnp.zeros((8, 128), jnp.float32)
+
+    for i in range(1, teams):
+        team_copy(0, i, team).start()
     own_copy.start()
 
     for hop in range(length - 1):
-        for c in range(CHUNKS):
+        for c in range(PARTS):
             for way in range(2):
                 at, there = behind(way, hop)
                 origin = at * 2 + core
@@ -460,7 +432,7 @@
             place_copy(back, i, place).wait_send()
     for i in range(1, teams):
         team_copy(1, i, mate(teams - i)[0]).wait_recv()
-    for c in range(CHUNKS):
+    for c in range(PARTS):
         pair(0, c, space, True).wait_send()
         pair(0, c, place * 2 + 1 - core, False).wait_recv()
         for way in range(2):
@@ -486,39 +458,59 @@
                     pair(index, c, at * 2 + 1 - core, False).wait_recv()
 
 
-def exchange(feat_grad, grads, space_size, member_size):
+def exchange(
+    features, wet_mask, target, w_in, w_out, scale_in, scale_out, space_size, member_size
+):
+    ocean_blocks, channels, cells = features.shape
+    hidden, outputs = w_out.shape
+    group = math.gcd(ocean_blocks // PARTS, 4)
+    padded = jnp.pad(w_out, ((0, 0), (0, 8 - outputs)))
     teams, length = 2 * member_size, space_size // 2
     hops = length - 1
-    piece = grads.shape[1:]
+    piece = (8, hidden + 128)
     dma = pltpu.SemaphoreType.DMA
     anywhere = pl.BlockSpec(memory_space=pl.ANY)
     return pl.pallas_call(
-        lambda *refs: exchange_kernel(space_size, member_size, *refs),
+        lambda *refs: exchange_kernel(space_size, member_size, scale_in, scale_out, *refs),
         out_shape=(
-            jax.ShapeDtypeStruct((space_size,) + feat_grad.shape, feat_grad.dtype),
-            jax.ShapeDtypeStruct(grads.shape, grads.dtype),
+            jax.ShapeDtypeStruct((space_size,) + features.shape, features.dtype),
+            jax.ShapeDtypeStruct((channels // 8,) + piece, jnp.float32),
         ),
-        in_specs=[anywhere, pl.BlockSpec(memory_space=pltpu.VMEM)],
+        in_specs=[pl.BlockSpec(memory_space=pltpu.VMEM)] * 7,
         out_specs=(anywhere, anywhere),
         scratch_shapes=[
-            pltpu.VMEM((teams - 1, length) + piece, grads.dtype),
-            pltpu.VMEM((length,) + piece, grads.dtype),
-            pltpu.VMEM((length - 1,) + piece, grads.dtype),
-            pltpu.VMEM(piece, grads.dtype),
+            pltpu.VMEM(features.shape, features.dtype),
+            pltpu.VMEM((channels // 8,) + piece, jnp.float32),
+            pltpu.VMEM((channels, hidden), jnp.float32),
+            pltpu.VMEM((hidden, group * cells), jnp.float32),
+            pltpu.VMEM((hidden, group * cells), jnp.bfloat16),
+            pltpu.VMEM((32, hidden), jnp.float32),
+            pltpu.VMEM((teams - 1, length) + piece, jnp.float32),
+            pltpu.VMEM((length,) + piece, jnp.float32),
+            pltpu.VMEM((length - 1,) + piece, jnp.float32),
+            pltpu.VMEM(piece, jnp.float32),
             dma((2, teams - 1)),
             dma((2, teams - 1)),
             dma((2, length - 1)),
             dma((2, length - 1)),
-            dma((2, hops, CHUNKS)),
-            dma((2, hops, CHUNKS)),
-            dma((1 + 2 * hops, CHUNKS)),
-            dma((1 + 2 * hops, CHUNKS)),
+            dma((2, hops, PARTS)),
+            dma((2, hops, PARTS)),
+            dma((1 + 2 * hops, PARTS)),
+            dma((1 + 2 * hops, PARTS)),
             dma((2,)),
         ],
         compiler_params=pltpu.CompilerParams(
             collective_id=0, has_side_effects=True, vmem_limit_bytes=VMEM_BYTES
         ),
-    )(feat_grad, grads)
+    )(
+        features,
+        wet_mask.astype(jnp.float32)[:, None, :],
+        jnp.pad(target, ((0, 0), (0, 8 - outputs), (0, 0))),
+        w_in,
+        w_in.T,
+        padded.T,
+        jnp.concatenate([padded, padded, padded, jnp.zeros_like(padded)], axis=1),
+    )
 
 
 def spread_kernel(
@@ -750,7 +742,7 @@
     pieces_fit = channels == 8 * space_size * member_size and w_in.shape[1] <= 16 * channels
     columns = lax.axis_size("group") * member_size
     capacity = min(atm_blocks, max(2, 2 * atm_blocks * top_count // space_size))
-    if not pieces_fit or ocean_blocks % CHUNKS or atm_blocks % CHUNKS or capacity % columns:
+    if not pieces_fit or ocean_blocks % PARTS or atm_blocks % CHUNKS or capacity % columns:
         return general_body(
             atm_state, remap_tiles, dest_device, dest_block, wet_mask, target, w_in, w_out
         )
@@ -788,19 +780,16 @@
     cell_total = member_size * space_size * ocean_blocks * cells
     scale_in = math.sqrt(w_in.shape[1] / cell_total)
     scale_out = 1.0 / math.sqrt(cell_total)
-    feat_grad, grads = network(
+    features = features_of(
         states.reshape(space_size * atm_blocks, channels, cells),
         tiles.reshape(slot_total, cells, cells),
         state_at,
         received_ids,
-        wet_mask,
-        target[0],
-        w_in,
-        w_out,
-        scale_in,
-        scale_out,
-    )
-    gathered, summed = exchange(feat_grad, grads, space_size, member_size)
+        ocean_blocks,
+    )
+    gathered, summed = exchange(
+        features, wet_mask, target[0], w_in, w_out, scale_in, scale_out, space_size, member_size
+    )
     owner = dest_flat * ocean_blocks + dest_block.reshape(pair_count)
     adjoint = adjoint_of(
         owner, gathered.reshape(space_size * ocean_blocks, channels, cells), remap_tiles

time: 200 us -> 186 us (0.930)
  Pallas kernels: 186 us -> 170 us
  local copies, waits for them, and re-layouts: 11 us -> 13.2 us
    pallas_call x2, Pallas kernels: 111 us -> 95 us  [the longest x1 88.7 us: exchange(): pl.pallas_call(lambda *refs: exchange_kernel(space_size, member_size, sca...]
    unnamed x13 -> x15, local copies, waits for them, and re-layouts: 6.21 us -> 8.39 us
where the time goes in v5:
time: 186 us
  Pallas kernels  170 us (91%)
  local copies, waits for them, and re-layouts  13.2 us (7%)
  other arithmetic  2 us (1%)
    pallas_call x1, Pallas kernels, exchange(): pl.pallas_call(lambda *refs: exchange_kernel(space_size, member_size, sca...  88.7 us
    pallas_call x1, Pallas kernels, spread(): pl.pallas_call(lambda *refs: spread_kernel(space_size, columns, member_si...  67.8 us
    unnamed x15, local copies, waits for them, and re-layouts  8.39 us
    pallas_call x1, Pallas kernels, features_of(): pl.pallas_call(features_kernel, out_shape=jax.ShapeDtypeStruct((ocean_blo...  6.36 us
    pallas_call x1, Pallas kernels, adjoint_of(): pl.pallas_call(adjoint_kernel, out_shape=jax.ShapeDtypeStruct((atm_blocks...  6.27 us

profile of v5, /device:TPU:0, one launch (start us, length us, event | category | flops | bytes accessed | tf_op | source)
XLA Modules:
  0.0 185.7 jit_solution(5242956778678241315)
XLA Ops:
  0.6 0.0 copy-start.5
  0.7 0.1 pad.18.clone
  0.7 0.7 broadcast_multiply_fusion
  1.5 0.1 add.77
  1.5 0.1 add.78
  1.6 0.1 copy.25
  1.7 0.1 mul.49
  1.8 0.8 copy.24
  2.6 0.1 reshape.81
  2.6 0.8 copy.23
  3.4 0.1 reshape.80
  3.5 0.7 convert_element_type.11
  4.2 0.1 fusion
  4.3 0.1 reduce_window_sum.11
  4.4 0.2 select_reduce_fusion
  4.6 0.8 scatter_custom_fusion
  5.4 0.1 reshape.82
  5.5 0.1 add_select_fusion
  5.5 0.1 reshape.83.pair_ref
  5.7 0.7 fusion.6
  6.4 0.1 maximum_maximum_fusion
  6.4 0.9 pad.13.refs_2_
  7.3 0.2 copy.27.refs_6_
  7.5 1.1 copy.26
  8.6 0.0 copy-start
  8.6 1.6 copy-done
  10.2 0.6 shard_map.103
  10.8 0.0 copy-done.5
  10.9 67.8 %shard_map.104 = (bf16[8,16,128,128]{3,2,1,0:T(8,128)(2,1)S(1)}, bf16[8,16,128,128]{3,2,1,0:T(8,128)(2,1)}, s32[8,8,128]{2,1,0:T(8,128)S(1)}) custom-call(bf16[16,128,128]{2,1,0:T(8,128)(2,1)S(1)} %bitcast.29, bf16[8,4,128,128]{3,2,1,0:T(8,128)(2,1)S(1)} %bitcast.27, s32[8,8,128]{2,1,0:T(8,128)S(1)} %broadcast_in_dim.22.refs_2_), custom_call_target="tpu_custom_call" | custom-call | tf_op jit(solution)/shard_map/pallas_call | solution.py:708
  78.6 0.0 copy-start.2
  78.6 2.0 %copy-done.2 = bf16[8,16,128,128]{3,2,1,0:T(8,128)(2,1)} copy-done((bf16[8,16,128,128]{3,2,1,0:T(8,128)(2,1)}, bf16[8,16,128,128]{3,2,1,0:T(8,128)(2,1)S(1)}, u32[]{:S(2)}) %copy-start.2) | copy-done | bytes 4194328
  80.6 0.1 squeeze.10
  80.7 0.0 copy-start.3
  80.7 2.2 %copy-done.3 = bf16[8,16,128,128]{3,2,1,0:T(8,128)(2,1)S(1)} copy-done((bf16[8,16,128,128]{3,2,1,0:T(8,128)(2,1)S(1)}, bf16[8,16,128,128]{3,2,1,0:T(8,128)(2,1)}, u32[]{:S(2)}) %copy-start.3) | copy-done | bytes 4194328
  82.9 0.0 copy-start.4
  82.9 0.0 copy-start.1
  82.9 6.4 %shard_map.105.refs_0_ = bf16[32,128,128]{2,1,0:T(8,128)(2,1)S(1)} custom-call(s32[128]{0:T(128)S(1)} %get-tuple-element.16.id_ref, s32[128]{0:T(128)S(1)} %get-tuple-element.15.state_at_ref, bf16[128,128,128]{2,1,0:T(8,128)(2,1)S(1)} %bitcast.26, bf16[128,128,128]{2,1,0:T(8,128)(2,1)} %bitcast.32), custom_call_target="tpu_custom_call" | custom-call | tf_op jit(solution)/shard_map/pallas_call | solution.py:179
  89.3 0.0 copy-done.4
  89.3 88.7 %shard_map.106 = (bf16[8,32,128,128]{3,2,1,0:T(8,128)(2,1)}, f32[16,8,1152]{2,1,0:T(8,128)S(1)}) custom-call(bf16[32,128,128]{2,1,0:T(8,128)(2,1)S(1)} %shard_map.105.refs_0_, f32[32,1,128]{2,1,0:T(1,128)S(1)} %bitcast.30, f32[32,8,128]{2,1,0:T(8,128)S(1)} %pad.13.refs_2_, bf16[128,1024]{1,0:T(8,128)(2,1)S(1)} %copy-done.4, bf16[1024,128]{1,0:T(8,128)(2,1)S(1)} %bitcast.28, ...), custom_call_target="tpu_custom_call" | custom-call | tf_op jit(solution)/shard_map/pallas_call | solution.py:473
  178.0 0.0 copy-done.1
  178.0 6.3 %shard_map.107 = f32[16,128,128]{2,1,0:T(8,128)} custom-call(s32[64]{0:T(128)S(1)} %get-tuple-element.18.slot_ref, bf16[256,128,128]{2,1,0:T(8,128)(2,1)} %bitcast.31, bf16[16,4,128,128]{3,2,1,0:T(8,128)(2,1)S(1)} %copy-done.1), custom_call_target="tpu_custom_call" | custom-call | tf_op jit(solution)/shard_map/pallas_call | solution.py:140
  184.2 0.6 slice_bitcast_fusion.1
  184.9 0.8 slice_bitcast_fusion
  (8 shorter events, 0.1 us)
Async XLA Ops:
  0.6 10.2 %copy-start.5 = (bf16[1,16,128,128]{3,2,1,0:T(8,128)(2,1)S(1)}, bf16[1,16,128,128]{3,2,1,0:T(8,128)(2,1)}, u32[]{:S(2)}) copy-start(bf16[1,16,128,128]{3,2,1,0:T(8,128)(2,1)} %param.8) | copy-start | bytes 1572868
  8.6 1.6 copy-start
  78.6 2.0 %copy-start.2 = (bf16[8,16,128,128]{3,2,1,0:T(8,128)(2,1)}, bf16[8,16,128,128]{3,2,1,0:T(8,128)(2,1)S(1)}, u32[]{:S(2)}) copy-start(bf16[8,16,128,128]{3,2,1,0:T(8,128)(2,1)S(1)} %get-tuple-element.9) | copy-start | bytes 12582916
  80.7 2.2 %copy-start.3 = (bf16[8,16,128,128]{3,2,1,0:T(8,128)(2,1)S(1)}, bf16[8,16,128,128]{3,2,1,0:T(8,128)(2,1)}, u32[]{:S(2)}) copy-start(bf16[8,16,128,128]{3,2,1,0:T(8,128)(2,1)} %copy-done.2) | copy-start | bytes 12582916
  82.9 6.4 %copy-start.4 = (bf16[128,1024]{1,0:T(8,128)(2,1)S(1)}, bf16[128,1024]{1,0:T(8,128)(2,1)}, u32[]{:S(2)}) copy-start(bf16[128,1024]{1,0:T(8,128)(2,1)} %refs_3_.1) | copy-start | bytes 786436
  82.9 95.1 %copy-start.1 = (bf16[16,4,128,128]{3,2,1,0:T(8,128)(2,1)S(1)}, bf16[16,4,128,128]{3,2,1,0:T(8,128)(2,1)}, u32[]{:S(2)}) copy-start(bf16[16,4,128,128]{3,2,1,0:T(8,128)(2,1)} %tiles_ref.1) | copy-start | bytes 6291460

commit v6 on v5

--- a/solution.py
+++ b/solution.py
@@ -620,7 +620,8 @@
         return at, (at >= 0 if way == 0 else at < length)
 
     ahead = (place < length - 1, place > 0)
-    for j in range(1, space_size):
+    order = sorted(range(1, space_size), key=lambda j: min(j, space_size - j))
+    for j in order:
         code(j, space).start()
         tile(j, space).start()
     own_codes = pltpu.make_async_copy(codes_ref.at[space], all_codes_ref.at[space], own_sem.at[2])
@@ -640,7 +641,6 @@
     own_state.start()
     own_tiles.start()
 
-    order = list(range(1, space_size))
     hops = length - 1
     for hop in range(hops):
         for j in order[hop * len(order) // hops : (hop + 1) * len(order) // hops]:

time: 186 us -> 186 us (level)
  no operation moved by 1% of the time
where the time goes in v6:
time: 186 us
  Pallas kernels  170 us (91%)
  local copies, waits for them, and re-layouts  13.2 us (7%)
  other arithmetic  2 us (1%)
    pallas_call x1, Pallas kernels, exchange(): pl.pallas_call(lambda *refs: exchange_kernel(space_size, member_size, sca...  88.7 us
    pallas_call x1, Pallas kernels, spread(): pl.pallas_call(lambda *refs: spread_kernel(space_size, columns, member_si...  67.7 us
    unnamed x15, local copies, waits for them, and re-layouts  8.39 us
    pallas_call x1, Pallas kernels, features_of(): pl.pallas_call(features_kernel, out_shape=jax.ShapeDtypeStruct((ocean_blo...  6.36 us
    pallas_call x1, Pallas kernels, adjoint_of(): pl.pallas_call(adjoint_kernel, out_shape=jax.ShapeDtypeStruct((atm_blocks...  6.27 us

profile of v6, /device:TPU:0, one launch (start us, length us, event | category | flops | bytes accessed | tf_op | source)
XLA Modules:
  0.0 185.6 jit_solution(3878695997649488873)
XLA Ops:
  0.6 0.0 copy-start.5
  0.7 0.1 pad.18.clone
  0.7 0.7 broadcast_multiply_fusion
  1.5 0.1 add.77
  1.5 0.1 add.78
  1.6 0.1 copy.25
  1.7 0.1 mul.49
  1.8 0.8 copy.24
  2.6 0.1 reshape.81
  2.6 0.8 copy.23
  3.4 0.1 reshape.80
  3.5 0.7 convert_element_type.11
  4.2 0.1 fusion
  4.3 0.1 reduce_window_sum.11
  4.4 0.2 select_reduce_fusion
  4.6 0.8 scatter_custom_fusion
  5.4 0.1 reshape.82
  5.5 0.1 add_select_fusion
  5.5 0.1 reshape.83.pair_ref
  5.7 0.7 fusion.6
  6.4 0.1 maximum_maximum_fusion
  6.4 0.9 pad.13.refs_2_
  7.3 0.2 copy.27.refs_6_
  7.5 1.1 copy.26
  8.6 0.0 copy-start
  8.6 1.6 copy-done
  10.2 0.6 shard_map.103
  10.8 0.0 copy-done.5
  10.9 67.7 %shard_map.104 = (bf16[8,16,128,128]{3,2,1,0:T(8,128)(2,1)S(1)}, bf16[8,16,128,128]{3,2,1,0:T(8,128)(2,1)}, s32[8,8,128]{2,1,0:T(8,128)S(1)}) custom-call(bf16[16,128,128]{2,1,0:T(8,128)(2,1)S(1)} %bitcast.29, bf16[8,4,128,128]{3,2,1,0:T(8,128)(2,1)S(1)} %bitcast.27, s32[8,8,128]{2,1,0:T(8,128)S(1)} %broadcast_in_dim.22.refs_2_), custom_call_target="tpu_custom_call" | custom-call | tf_op jit(solution)/shard_map/pallas_call | solution.py:708
  78.6 0.0 copy-start.2
  78.6 2.0 %copy-done.2 = bf16[8,16,128,128]{3,2,1,0:T(8,128)(2,1)} copy-done((bf16[8,16,128,128]{3,2,1,0:T(8,128)(2,1)}, bf16[8,16,128,128]{3,2,1,0:T(8,128)(2,1)S(1)}, u32[]{:S(2)}) %copy-start.2) | copy-done | bytes 4194328
  80.6 0.1 squeeze.10
  80.7 0.0 copy-start.3
  80.7 2.2 %copy-done.3 = bf16[8,16,128,128]{3,2,1,0:T(8,128)(2,1)S(1)} copy-done((bf16[8,16,128,128]{3,2,1,0:T(8,128)(2,1)S(1)}, bf16[8,16,128,128]{3,2,1,0:T(8,128)(2,1)}, u32[]{:S(2)}) %copy-start.3) | copy-done | bytes 4194328
  82.9 0.0 copy-start.4
  82.9 0.0 copy-start.1
  82.9 6.4 %shard_map.105.refs_0_ = bf16[32,128,128]{2,1,0:T(8,128)(2,1)S(1)} custom-call(s32[128]{0:T(128)S(1)} %get-tuple-element.16.id_ref, s32[128]{0:T(128)S(1)} %get-tuple-element.15.state_at_ref, bf16[128,128,128]{2,1,0:T(8,128)(2,1)S(1)} %bitcast.26, bf16[128,128,128]{2,1,0:T(8,128)(2,1)} %bitcast.32), custom_call_target="tpu_custom_call" | custom-call | tf_op jit(solution)/shard_map/pallas_call | solution.py:179
  89.2 0.0 copy-done.4
  89.2 88.7 %shard_map.106 = (bf16[8,32,128,128]{3,2,1,0:T(8,128)(2,1)}, f32[16,8,1152]{2,1,0:T(8,128)S(1)}) custom-call(bf16[32,128,128]{2,1,0:T(8,128)(2,1)S(1)} %shard_map.105.refs_0_, f32[32,1,128]{2,1,0:T(1,128)S(1)} %bitcast.30, f32[32,8,128]{2,1,0:T(8,128)S(1)} %pad.13.refs_2_, bf16[128,1024]{1,0:T(8,128)(2,1)S(1)} %copy-done.4, bf16[1024,128]{1,0:T(8,128)(2,1)S(1)} %bitcast.28, ...), custom_call_target="tpu_custom_call" | custom-call | tf_op jit(solution)/shard_map/pallas_call | solution.py:473
  177.9 0.0 copy-done.1
  177.9 6.3 %shard_map.107 = f32[16,128,128]{2,1,0:T(8,128)} custom-call(s32[64]{0:T(128)S(1)} %get-tuple-element.18.slot_ref, bf16[256,128,128]{2,1,0:T(8,128)(2,1)} %bitcast.31, bf16[16,4,128,128]{3,2,1,0:T(8,128)(2,1)S(1)} %copy-done.1), custom_call_target="tpu_custom_call" | custom-call | tf_op jit(solution)/shard_map/pallas_call | solution.py:140
  184.2 0.6 slice_bitcast_fusion.1
  184.8 0.8 slice_bitcast_fusion
  (8 shorter events, 0.1 us)
Async XLA Ops:
  0.6 10.2 %copy-start.5 = (bf16[1,16,128,128]{3,2,1,0:T(8,128)(2,1)S(1)}, bf16[1,16,128,128]{3,2,1,0:T(8,128)(2,1)}, u32[]{:S(2)}) copy-start(bf16[1,16,128,128]{3,2,1,0:T(8,128)(2,1)} %param.8) | copy-start | bytes 1572868
  8.6 1.6 copy-start
  78.6 2.0 %copy-start.2 = (bf16[8,16,128,128]{3,2,1,0:T(8,128)(2,1)}, bf16[8,16,128,128]{3,2,1,0:T(8,128)(2,1)S(1)}, u32[]{:S(2)}) copy-start(bf16[8,16,128,128]{3,2,1,0:T(8,128)(2,1)S(1)} %get-tuple-element.9) | copy-start | bytes 12582916
  80.7 2.2 %copy-start.3 = (bf16[8,16,128,128]{3,2,1,0:T(8,128)(2,1)S(1)}, bf16[8,16,128,128]{3,2,1,0:T(8,128)(2,1)}, u32[]{:S(2)}) copy-start(bf16[8,16,128,128]{3,2,1,0:T(8,128)(2,1)} %copy-done.2) | copy-start | bytes 12582916
  82.9 6.4 %copy-start.4 = (bf16[128,1024]{1,0:T(8,128)(2,1)S(1)}, bf16[128,1024]{1,0:T(8,128)(2,1)}, u32[]{:S(2)}) copy-start(bf16[128,1024]{1,0:T(8,128)(2,1)} %refs_3_.1) | copy-start | bytes 786436
  82.9 95.1 %copy-start.1 = (bf16[16,4,128,128]{3,2,1,0:T(8,128)(2,1)S(1)}, bf16[16,4,128,128]{3,2,1,0:T(8,128)(2,1)}, u32[]{:S(2)}) copy-start(bf16[16,4,128,128]{3,2,1,0:T(8,128)(2,1)} %tiles_ref.1) | copy-start | bytes 6291460
